TPU v7x, 256 devices: a whole 4x4x8 slice. The times are simulated.
256 devices in a mesh: dp: 4 (over x), segment: 2 (over core), band: 32 (over z, y).
Axes of the slice: x: 4, y: 4, z: 8, core: 2. Of those that a mesh axis runs over, the one named last changes fastest.
Arguments:
- fields: bfloat16 [4, 2, 256, 16, 512], P('dp', None, 'band'), may hold values from -6 to 6
- cell_mask: int32 [4, 2, 256, 16], P('dp', None, 'band'), may hold values 0 or 1
- merge_weight: bfloat16 [2, 1024, 512], P('segment', 'dp'), may hold values from -0.1875 to 0.1875
- qkv_weight: bfloat16 [2, 512, 1536], P('segment', 'dp')
- out_weight: bfloat16 [2, 512, 512], P('segment', 'dp'), may hold values from -1 to 1
- norm_gain: bfloat16 [2, 512], P('segment', 'dp'), may hold values from 0.099609375 to 1.8984375
- out_cotangent: bfloat16 [4, 2, 256, 16, 512], P('dp', None, 'band'), may hold values from -6 to 6
Outputs:
- section_out: bfloat16 [2, 4, 2, 256, 16, 512], P('segment', 'dp', None, 'band')
- merge_grad: float32 [2, 1024, 512], P('segment', 'dp')
- qkv_grad: float32 [2, 512, 1536], P('segment', 'dp')
- out_grad: float32 [2, 512, 512], P('segment', 'dp')
- gain_grad: float32 [2, 512], P('segment', 'dp')
Inputs may be any that keep to these rules, and one draw needn't show every extreme that they name: `cell_mask`: 1 marks a cell whose keys may be attended.
All inputs are finite; a program needn't handle non-finite values. No bound on the sum of `cell_mask` on one device may be relied on, other than what follows from the above.
Results may differ from a plain program's by a relative error of at most 0.03.
Values may be sent and summed in bfloat16 or wider, within the bound.
A program may use at most 128 MiB of HBM per device.

v0:
```python
from functools import partial

import jax
import jax.numpy as jnp
from jax import lax
from jax.sharding import PartitionSpec as P

HEADS = 8
WH = 8
WW = 16
SH = 4
SW = 8


EPSILON = 1e-05
MASKED = -1e30


def padded(shard, sides, width):
    for axis, dim in sides:
        size, length = (lax.axis_size(axis), shard.shape[dim])
        up = [(i, (i + 1) % size) for i in range(size - 1)]
        down = [(j, i) for i, j in up]
        last = lax.slice_in_dim(shard, length - width, length, axis=dim)
        first = lax.slice_in_dim(shard, 0, width, axis=dim)
        before = lax.ppermute(last, axis, up)
        after = lax.ppermute(first, axis, down)
        shard = jnp.concatenate([before, shard, after], axis=dim)
    return shard


def partner(shard, axis, distance):
    return lax.ppermute(shard, axis, [(i, i ^ 1 << distance) for i in range(lax.axis_size(axis))])


def normalize(update):
    average = jnp.mean(update, axis=-1, keepdims=True)
    centered = update - average
    spread = jnp.mean(centered * centered, axis=-1, keepdims=True)
    inverse = lax.rsqrt(spread + EPSILON)
    return (centered * inverse, inverse)


def window_pattern(lon_count):
    query_index = jnp.arange(WH * lon_count, dtype=jnp.int32)
    key_index = jnp.arange(2 * WH * lon_count, dtype=jnp.int32)
    query_row = query_index // lon_count
    query_col = query_index % lon_count
    key_row = key_index // lon_count
    key_col = key_index % lon_count
    lat_same = ((query_row + SH) // WH)[:, None] == (key_row // WH)[None, :]
    lon_same = ((query_col + SW) // WW)[:, None] == ((key_col + SW) // WW)[None, :]
    self_key = ((query_row + SH)[:, None] == key_row[None, :]) & (
        query_col[:, None] == key_col[None, :]
    )
    return (lat_same & lon_same, self_key)


def attend(queries, keyvals, usable):
    row_count, lon_count, feature = queries.shape
    blocks = row_count // WH
    head_dim = feature // HEADS
    query_blocks = queries.reshape(blocks, WH * lon_count, HEADS, head_dim)
    kv_blocks = keyvals.reshape(blocks + 1, WH * lon_count, 2, HEADS, head_dim)
    key_pairs = jnp.concatenate([kv_blocks[:-1], kv_blocks[1:]], axis=1)
    use_blocks = usable.reshape(blocks + 1, WH * lon_count)
    use_pairs = jnp.concatenate([use_blocks[:-1], use_blocks[1:]], axis=1)
    inside, self_key = window_pattern(lon_count)
    allowed = inside[None] & (use_pairs[:, None, :] | self_key[None])
    scores = jnp.einsum(
        "nqhd,nkhd->nhqk", query_blocks, key_pairs[:, :, 0], preferred_element_type=jnp.float32
    ) * head_dim ** (-0.5)
    scores = jnp.where(allowed[:, None], scores, MASKED)
    highest = jnp.max(scores, axis=-1, keepdims=True)
    weights = jnp.exp(scores - highest)
    attn_prob = (weights / jnp.sum(weights, axis=-1, keepdims=True)).astype(jnp.bfloat16)
    mixture = jnp.einsum(
        "nhqk,nkhd->nqhd", attn_prob, key_pairs[:, :, 1], preferred_element_type=jnp.float32
    )
    return mixture.reshape(row_count, lon_count, feature).astype(jnp.bfloat16)


def guarded(active, function, operands):

    def skipped(values):
        return jax.tree.map(jnp.zeros_like, function(values))

    return lax.cond(active, function, skipped, operands)


def project(joined, merge_full, qkv_full, gain_full):
    update = jnp.einsum("rwj,jd->rwd", joined, merge_full, preferred_element_type=jnp.float32)
    normed, inverse = normalize(update)
    hidden = (normed * gain_full.astype(jnp.float32)).astype(jnp.bfloat16)
    projected = jnp.einsum("rwd,de->rwe", hidden, qkv_full, preferred_element_type=jnp.float32)
    feature = update.shape[-1]
    queries = projected[..., :feature].astype(jnp.bfloat16)
    keyvals = projected[..., feature:].astype(jnp.bfloat16)
    return (update, normed, inverse, hidden, queries, keyvals)


def section_forward(active, joined, usable, merge_full, qkv_full, gain_full, out_full):
    update, normed, inverse, hidden, queries, own_keys = guarded(
        active, lambda rows_own: project(rows_own, merge_full, qkv_full, gain_full), joined
    )
    keyvals = padded(own_keys, (("band", 0),), SH)

    def finish(operands):
        update_in, query_in, keyval_in, usable_in = operands
        mixture = attend(query_in, keyval_in, usable_in)
        result = (
            update_in
            + jnp.einsum("rwd,de->rwe", mixture, out_full, preferred_element_type=jnp.float32)
        ).astype(jnp.bfloat16)
        return (mixture, result)

    mixture, result = guarded(active, finish, (update, queries, keyvals, usable))
    return (result, (joined, normed, inverse, hidden, queries, keyvals, mixture))


def attend_back(out_full, operands):
    grad_out, queries, keyvals, mixture, usable = operands
    grad_mixture = jnp.einsum(
        "rwe,de->rwd", grad_out, out_full, preferred_element_type=jnp.float32
    ).astype(jnp.bfloat16)
    unused, pull_back = jax.vjp(
        lambda query_in, keyval_in: attend(query_in, keyval_in, usable), queries, keyvals
    )
    grad_query, grad_keyval = pull_back(grad_mixture)
    grad_outw = jnp.einsum("rwd,rwe->de", mixture, grad_out, preferred_element_type=jnp.float32)
    return (grad_query, grad_keyval, grad_outw)


def fold_rims(grad_keyval, row_count):
    rim_rows = jnp.concatenate([grad_keyval[:SH], grad_keyval[SH + row_count :]], axis=0)
    returned = padded(rim_rows, (("band", 0),), SH)
    own_part = grad_keyval[SH : SH + row_count].astype(jnp.float32)
    return jnp.concatenate(
        [
            own_part[:SH] + returned[:SH].astype(jnp.float32),
            own_part[SH : row_count - SH],
            own_part[row_count - SH :] + returned[3 * SH :].astype(jnp.float32),
        ],
        axis=0,
    ).astype(jnp.bfloat16)


def back_core(qkv_full, gain_full, grad_query, grad_keyown, grad_out, normed, inverse):
    grad_proj = jnp.concatenate([grad_query, grad_keyown], axis=-1)
    grad_hidden = jnp.einsum("rwe,de->rwd", grad_proj, qkv_full, preferred_element_type=jnp.float32)
    grad_normed = grad_hidden * gain_full.astype(jnp.float32)
    grad_update = (
        grad_out.astype(jnp.float32)
        + inverse
        * (
            grad_normed
            - jnp.mean(grad_normed, axis=-1, keepdims=True)
            - normed * jnp.mean(grad_normed * normed, axis=-1, keepdims=True)
        )
    ).astype(jnp.bfloat16)
    return (grad_proj, grad_hidden, grad_update)


def project_back(merge_part, qkv_full, gain_full, operands):
    grad_query, grad_keyown, grad_out, joined, normed, inverse, hidden = operands
    grad_proj, grad_hidden, grad_update = back_core(
        qkv_full, gain_full, grad_query, grad_keyown, grad_out, normed, inverse
    )
    grad_qkv = jnp.einsum("rwd,rwe->de", hidden, grad_proj, preferred_element_type=jnp.float32)
    grad_gain = jnp.sum(grad_hidden * normed, axis=(0, 1))
    grad_merge = jnp.einsum("rwj,rwd->jd", joined, grad_update, preferred_element_type=jnp.float32)
    grad_joined = jnp.einsum(
        "rwd,jd->rwj", grad_update, merge_part, preferred_element_type=jnp.float32
    )
    return (grad_joined, grad_merge, grad_qkv, grad_gain)


def store_slot(buffers, values, slot_index, active):

    def place_one(buffer, new_value):
        current = lax.dynamic_index_in_dim(buffer, slot_index, 0, keepdims=False)
        return lax.dynamic_update_index_in_dim(
            buffer, jnp.where(active, new_value, current), slot_index, 0
        )

    return jax.tree.map(place_one, buffers, values)


def body(fields, cell_mask, merge_weight, qkv_weight, out_weight, norm_gain, out_cotangent):
    merge_rows, qkv_rows, out_rows, gain_rows = (
        lax.all_gather(merge_weight, "dp", axis=1, tiled=True),
        lax.all_gather(qkv_weight, "dp", axis=1, tiled=True),
        lax.all_gather(out_weight, "dp", axis=1, tiled=True),
        lax.all_gather(norm_gain, "dp", axis=1, tiled=True),
    )
    merge_full = merge_rows[0]
    qkv_full = qkv_rows[0]
    out_full = out_rows[0]
    gain_full = gain_rows[0]
    inputs = fields[0]
    cotangent = out_cotangent[0]
    micro_count, row_count, lon_count, feature = inputs.shape
    mask_ext = padded(cell_mask[0], (("band", 1),), SH)
    usable_ext = mask_ext == 1
    section_count = lax.axis_size("segment")
    half_count = section_count // 2
    section_rank = lax.axis_index("segment")
    tick_count = half_count + micro_count - 1

    def to_partner(payload):
        payload = partner(payload, "segment", 0)
        return payload

    def forward_tick(phase, feed):

        def forward_one_tick(tick_index, state_in):
            sending, section_buf, stashed = state_in
            rank_local = section_rank - phase * half_count
            micro_index = tick_index - rank_local
            active = (
                (rank_local >= 0)
                & (rank_local < half_count)
                & (micro_index >= 0)
                & (micro_index < micro_count)
            )
            slot_index = jnp.clip(micro_index, 0, micro_count - 1)
            feed_now = lax.dynamic_index_in_dim(feed, slot_index, 0, keepdims=False)
            joined = jnp.concatenate([feed_now, feed_now], axis=-1)
            usable = lax.dynamic_index_in_dim(usable_ext, slot_index, 0, keepdims=False)
            result, record = section_forward(
                active, joined, usable, merge_full, qkv_full, gain_full, out_full
            )
            section_buf = store_slot(section_buf, result, slot_index, active)
            stashed = store_slot(stashed, record, slot_index, active)
            return (result, section_buf, stashed)

        return forward_one_tick

    def backward_tick(phase, feed, stashed):
        merge_part = merge_full if phase == 0 else merge_full[:feature]

        def backward_one_tick(tick_index, state_in):
            sending, skip_buf, grad_sums = state_in
            rank_local = section_count - 1 - section_rank - phase * half_count
            micro_index = tick_index - rank_local
            active = (
                (rank_local >= 0)
                & (rank_local < half_count)
                & (micro_index >= 0)
                & (micro_index < micro_count)
            )
            slot_index = jnp.clip(micro_index, 0, micro_count - 1)
            grad_out = lax.dynamic_index_in_dim(feed, slot_index, 0, keepdims=False)
            joined, normed, inverse, hidden, queries, keyvals, mixture = jax.tree.map(
                lambda buffer: lax.dynamic_index_in_dim(buffer, slot_index, 0, keepdims=False),
                stashed,
            )
            usable = lax.dynamic_index_in_dim(usable_ext, slot_index, 0, keepdims=False)
            grad_query, grad_keyval, grad_outw = guarded(
                active,
                partial(attend_back, out_full),
                (grad_out, queries, keyvals, mixture, usable),
            )
            grad_keyown = fold_rims(grad_keyval, row_count)
            grad_joined, grad_merge, grad_qkv, grad_gain = guarded(
                active,
                partial(project_back, merge_part, qkv_full, gain_full),
                (grad_query, grad_keyown, grad_out, joined, normed, inverse, hidden),
            )
            grad_sums = (
                grad_sums[0] + grad_merge,
                grad_sums[1] + grad_qkv,
                grad_sums[2] + grad_outw,
                grad_sums[3] + grad_gain,
            )
            grad_chain = grad_joined[..., :feature].astype(jnp.bfloat16)
            if phase == 0:
                grad_side = grad_joined[..., feature:].astype(jnp.bfloat16)
                toward = jnp.where(
                    section_rank == half_count,
                    (grad_chain.astype(jnp.float32) + grad_side.astype(jnp.float32)).astype(
                        jnp.bfloat16
                    ),
                    grad_side,
                )
                skip_buf = store_slot(skip_buf, toward, slot_index, active)
            return (grad_chain, skip_buf, grad_sums)

        return backward_one_tick

    stashed = (
        jnp.zeros((micro_count, row_count, lon_count, 2 * feature), jnp.bfloat16),
        jnp.zeros((micro_count, row_count, lon_count, feature), jnp.float32),
        jnp.zeros((micro_count, row_count, lon_count, 1), jnp.float32),
        jnp.zeros((micro_count, row_count, lon_count, feature), jnp.bfloat16),
        jnp.zeros((micro_count, row_count, lon_count, feature), jnp.bfloat16),
        jnp.zeros((micro_count, row_count + 2 * SH, lon_count, 2 * feature), jnp.bfloat16),
        jnp.zeros((micro_count, row_count, lon_count, feature), jnp.bfloat16),
    )
    section_buf = jnp.zeros((micro_count, row_count, lon_count, feature), jnp.bfloat16)
    spare_rows = jnp.zeros((row_count, lon_count, feature), jnp.bfloat16)
    unused, section_buf, stashed = lax.fori_loop(
        0, tick_count, forward_tick(0, inputs), (spare_rows, section_buf, stashed)
    )
    skip_in = to_partner(section_buf)
    unused, section_buf, stashed = lax.fori_loop(
        0, tick_count, forward_tick(1, skip_in), (spare_rows, section_buf, stashed)
    )
    grad_sums = (
        jnp.zeros((2 * feature, feature), jnp.float32),
        jnp.zeros((feature, 3 * feature), jnp.float32),
        jnp.zeros((feature, feature), jnp.float32),
        jnp.zeros((feature,), jnp.float32),
    )
    unused, skip_buf, grad_sums = lax.fori_loop(
        0,
        tick_count,
        backward_tick(0, cotangent, stashed),
        (spare_rows, jnp.zeros_like(section_buf), grad_sums),
    )
    skip_back = to_partner(skip_buf)
    unused, skip_buf, grad_sums = lax.fori_loop(
        0, tick_count, backward_tick(1, skip_back, stashed), (spare_rows, skip_buf, grad_sums)
    )
    section_home = section_buf[None, None]
    merge_part_sum, qkv_part_sum, out_part_sum, gain_part_sum = (
        lax.psum_scatter(
            grad_sums[0][None].astype(jnp.bfloat16), "dp", scatter_dimension=1, tiled=True
        ).astype(jnp.float32),
        lax.psum_scatter(
            grad_sums[1][None].astype(jnp.bfloat16), "dp", scatter_dimension=1, tiled=True
        ).astype(jnp.float32),
        lax.psum_scatter(
            grad_sums[2][None].astype(jnp.bfloat16), "dp", scatter_dimension=1, tiled=True
        ).astype(jnp.float32),
        lax.psum_scatter(
            grad_sums[3][None].astype(jnp.bfloat16), "dp", scatter_dimension=1, tiled=True
        ).astype(jnp.float32),
    )
    merge_grad, qkv_grad, out_grad, gain_grad = (
        lax.psum(merge_part_sum.astype(jnp.bfloat16), "band").astype(jnp.float32),
        lax.psum(qkv_part_sum.astype(jnp.bfloat16), "band").astype(jnp.float32),
        lax.psum(out_part_sum.astype(jnp.bfloat16), "band").astype(jnp.float32),
        lax.psum(gain_part_sum.astype(jnp.bfloat16), "band").astype(jnp.float32),
    )
    return (section_home, merge_grad, qkv_grad, out_grad, gain_grad)


def solution(mesh):
    return jax.shard_map(
        body,
        mesh=mesh,
        in_specs=(
            P("dp", None, "band", None, None),
            P("dp", None, "band", None),
            P("segment", "dp", None),
            P("segment", "dp", None),
            P("segment", "dp", None),
            P("segment", "dp"),
            P("dp", None, "band", None, None),
        ),
        out_specs=(
            P("segment", "dp", None, "band", None, None),
            P("segment", "dp", None),
            P("segment", "dp", None),
            P("segment", "dp", None),
            P("segment", "dp"),
        ),
        check_vma=False,
    )
```

profile of v0, /device:TPU:2, one launch (start us, length us, event | category | flops | bytes accessed | tf_op | source)
XLA Modules:
  0.0 875.8 jit_solution(191999634789803929)
XLA Ops:
  14.3 13.6 %all_gather.15 = bf16[1,512,512]{2,1,0:T(8,128)(2,1)S(1)} all-gather(bf16[1,128,512]{2,1,0:T(8,128)(2,1)} %param.35), channel_id=1, replica_groups=mesh['dp'=4,'segment'=2,'band'=32] {'dp'}, dimensions={1}, use_global_device_ids=true | all-gather | bytes 655360 | tf_op jit(solution)/shard_map/all_gather | solution.py:193
  27.9 7.6 all_gather.13
  38.2 32.2 %all-gather.5.cloned.1.call-done = bf16[1,512,1536]{2,1,0:T(8,128)(2,1)} async-done(((bf16[1,128,1536]{2,1,0:T(8,128)(2,1)}), bf16[1,512,1536]{2,1,0:T(8,128)(2,1)}) %all-gather.5.cloned.1.call-update) | async-done | bytes 1572880 | tf_op jit(solution)/shard_map/all_gather | solution.py:192
  76.2 116.6 %while.103 = (s32[]{:T(128)}, bf16[2,8,16,512]{3,2,1,0:T(8,128)(2,1)}, bf16[2,8,16,1024]{3,2,1,0:T(8,128)(2,1)}, f32[2,8,16,512]{3,2,1,0:T(8,128)}, f32[2,8,16,1...) while((s32[]{:T(128)}, ...), condition=%wide.region_9.10_spmd, body=%wide.region_0.9_spmd.sunk | while | flops 477448448 | bytes 26721116 | solution.py:302
  77.2 5.2 conditional.18
  84.5 5.2 collective-permute-start.1
  103.1 27.5 %conditional.19 = (bf16[8,16,512]{2,1,0:T(8,128)(2,1)}, bf16[8,16,512]{2,1,0:T(8,128)(2,1)}) conditional(s32[]{:T(128)} %convert_element_type.561, () %tuple.323, (bf16[16,16,1024]{2,1,0:T(8,128)(2,1)}, pred[2,16,16]{2,1,0:T(8,128)(4,1)S(1)}, s32[]{:T(128)}, bf16[8,16,512]{2,1,0:T(8,128)(2,1)S(1)}, bf16[512,512]{1,0:T(8,128)(2,1)S(1)}, ...), branch_computations={%region_5.5_spmd, %region_6.8_spmd} | conditional | flops 137315840 | bytes 8476452 | solution.py:88
  135.4 5.2 conditional.18
  142.7 5.2 collective-permute-start.1
  161.4 27.5 %conditional.19 = (bf16[8,16,512]{2,1,0:T(8,128)(2,1)}, bf16[8,16,512]{2,1,0:T(8,128)(2,1)}) conditional(s32[]{:T(128)} %convert_element_type.561, () %tuple.323, (bf16[16,16,1024]{2,1,0:T(8,128)(2,1)}, pred[2,16,16]{2,1,0:T(8,128)(4,1)S(1)}, s32[]{:T(128)}, bf16[8,16,512]{2,1,0:T(8,128)(2,1)S(1)}, bf16[512,512]{1,0:T(8,128)(2,1)S(1)}, ...), branch_computations={%region_5.5_spmd, %region_6.8_spmd} | conditional | flops 137315840 | bytes 8476452 | solution.py:88
  194.7 54.8 %while.104 = (s32[]{:T(128)}, bf16[2,8,16,512]{3,2,1,0:T(8,128)(2,1)}, bf16[2,8,16,1024]{3,2,1,0:T(8,128)(2,1)}, f32[2,8,16,512]{3,2,1,0:T(8,128)}, f32[2,8,16,1...) while((s32[]{:T(128)}, ...), condition=%wide.region_19.20_spmd, body=%wide.region_10.19_spmd.sunk | while | flops 477448448 | bytes 26721116 | solution.py:306
  199.2 5.2 collective-permute-start.3
  226.6 5.2 collective-permute-start.3
  250.3 60.6 %while.106 = (s32[]{:T(128)}, bf16[2,8,16,512]{3,2,1,0:T(8,128)(2,1)}, f32[1024,512]{1,0:T(8,128)}, f32[512,1536]{1,0:T(8,128)}, f32[512,512]{1,0:T(8,128)}, /*i...) while((s32[]{:T(128)}, ...), condition=%wide.region_33.34_spmd.clone, body=%wide.region_20.33_spmd.clone.sunk | while | flops 992495872 | bytes 121524072 | solution.py:315
  255.1 4.3 collective-permute-start.6
  284.2 6.7 collective-permute-start.6
  303.3 4.3 select_add_fusion.8
  310.9 143.5 %collective-permute-start.11 = (bf16[2,8,16,512]{3,2,1,0:T(8,128)(2,1)}, bf16[2,8,16,512]{3,2,1,0:T(8,128)(2,1)S(1)}, u32[]{:S(2)}, u32[]{:S(2)}) collective-permute-start(bf16[2,8,16,512]{3,2,1,0:T(8,128)(2,1)} %get-tuple-element.2101), channel_id=1, source_target_pairs={{0,32},{32,0},{1,33},{33,1},{2,34},{34,2},{3,35},{35,3},{4,36},{36... | collective-permute-start | bytes 786440 | tf_op jit(solution)/shard_map/ppermute | solution.py:33
  455.8 131.6 %while.105 = (s32[]{:T(128)}, f32[1024,512]{1,0:T(8,128)}, f32[512,1536]{1,0:T(8,128)}, f32[512,512]{1,0:T(8,128)}, f32[512]{0:T(512)}, /*index=5*/s32[]{:T(128)...) while((s32[]{:T(128)}, f32[1024,512]{1,0:T(8,128)}, ...), condition=%wide.region_47.48_spmd, body=%wide.region_34.47_spmd.sunk | while | flops 856311552 | bytes 123788608 | solution.py:322
  456.6 35.0 %conditional.22 = (bf16[8,16,512]{2,1,0:T(8,128)(2,1)}, bf16[16,16,1024]{2,1,0:T(8,128)(2,1)}, f32[512,512]{1,0:T(8,128)}) conditional(s32[]{:T(128)} %convert_element_type.565, () %tuple.339, (pred[2,16,16]{2,1,0:T(8,128)(4,1)S(1)}, s32[]{:T(128)}, bf16[8,16,512]{2,1,0:T(8,128)(2,1)}, bf16[512,512]{1,0:T(8,128)(2,1)S(1)}, ...), branch_computations={%region_35.35_spmd, %region_36.41_spmd} | conditional | flops 316294400 | bytes 26212748 | solution.py:88
  492.6 6.2 collective-permute-start.4
  506.9 6.1 conditional.23
  514.7 4.3 add.947
  522.9 35.0 %conditional.22 = (bf16[8,16,512]{2,1,0:T(8,128)(2,1)}, bf16[16,16,1024]{2,1,0:T(8,128)(2,1)}, f32[512,512]{1,0:T(8,128)}) conditional(s32[]{:T(128)} %convert_element_type.565, () %tuple.339, (pred[2,16,16]{2,1,0:T(8,128)(4,1)S(1)}, s32[]{:T(128)}, bf16[8,16,512]{2,1,0:T(8,128)(2,1)}, bf16[512,512]{1,0:T(8,128)(2,1)S(1)}, ...), branch_computations={%region_35.35_spmd, %region_36.41_spmd} | conditional | flops 316294400 | bytes 26212748 | solution.py:88
  572.2 6.1 conditional.23
  580.0 4.3 add.947
  596.6 27.5 %reduce-scatter.11.cloned.1.call-done = bf16[1,128,512]{2,1,0:T(8,128)(2,1)} async-done(((bf16[1,512,512]{2,1,0:T(8,128)(2,1)}), bf16[1,128,512]{2,1,0:T(8,128)(2,1)}) %reduce-scatter.11.cloned.1.call-update) | async-done | bytes 131088 | tf_op jit(solution)/shard_map/reduce_scatter | solution.py:333
  624.1 28.4 %reduce-scatter.7.cloned.1.call-done = bf16[1,256,512]{2,1,0:T(8,128)(2,1)} async-done(((bf16[1,1024,512]{2,1,0:T(8,128)(2,1)}), bf16[1,256,512]{2,1,0:T(8,128)(2,1)}) %reduce-scatter.7.cloned.1.call-update) | async-done | bytes 262160 | tf_op jit(solution)/shard_map/reduce_scatter | solution.py:327
  652.5 31.1 %reduce-scatter.9.cloned.1.call-done = bf16[1,128,1536]{2,1,0:T(8,128)(2,1)} async-done(((bf16[1,512,1536]{2,1,0:T(8,128)(2,1)}), bf16[1,128,1536]{2,1,0:T(8,128)(2,1)}) %reduce-scatter.9.cloned.1.call-update) | async-done | bytes 393232 | tf_op jit(solution)/shard_map/reduce_scatter | solution.py:330
  683.6 25.3 %reduce-scatter.13.cloned.1.call-done = bf16[128,1]{1,0:T(8,128)(2,1)} async-done(((bf16[512,1]{1,0:T(8,128)(2,1)}), bf16[128,1]{1,0:T(8,128)(2,1)}) %reduce-scatter.13.cloned.1.call-update) | async-done | bytes 272
  709.8 75.3 %psum.31 = bf16[1,128]{1,0:T(2,128)(2,1)S(1)} all-reduce(bf16[1,128]{1,0:T(2,128)(2,1)S(1)} %copy.91), channel_id=1, replica_groups=mesh['dp'=4,'segment'=2,'band'=32] {'band'}, use_global_device_ids=true, to_apply=%region_55.56 | all-reduce | flops 128 | bytes 512 | tf_op jit(solution)/shard_map/psum | solution.py:344
  785.6 77.6 %all-reduce.11.cloned.1.call-done = (bf16[1,256,512]{2,1,0:T(8,128)(2,1)}, bf16[1,128,1536]{2,1,0:T(8,128)(2,1)}, bf16[1,128,512]{2,1,0:T(8,128)(2,1)}) async-done(((bf16[1,256,512]{2,1,0:T(8,128)(2,1)}, bf16[1,128,1536]{2,1,0:T(8,128)(2,1)}, bf16[1,128,512]{2,1,0:T(8,128)(2,1)}), (bf16[1,256,512]{2,1,0:T(8,128)(2,1)}, bf16[1,128,1536]{2,1,0:T(8,128)(2,1)}, ...) | async-done | bytes 786448 | tf_op jit(solution)/shard_map/psum | solution.py:341
  (498 shorter events, 359.9 us)
Async XLA Ops:
  7.2 31.1 %all-gather.3.cloned.1.call-start = ((), (), s32[]{:S(2)}) async-start(), calls=%async_computation.4 | async-start | bytes 1310720 | tf_op jit(solution)/shard_map/all_gather | solution.py:191
  7.9 62.5 %all-gather.5.cloned.1.call-start = ((), (), s32[]{:S(2)}) async-start(), calls=%async_computation.5 | async-start | bytes 1966080 | tf_op jit(solution)/shard_map/all_gather | solution.py:192
  8.6 615.4 %reduce-scatter.11.cloned.1.call-start = ((), (), s32[]{:S(2)}) async-start(), calls=%async_computation.8 | async-start | bytes 655360 | tf_op jit(solution)/shard_map/reduce_scatter | solution.py:333
  9.5 26.0 %collective-permute-start.8 = (s32[2,4,16]{2,1,0:T(4,128)S(1)}, s32[2,4,16]{2,1,0:T(4,128)S(1)}, u32[]{:S(2)}, u32[]{:S(2)}) collective-permute-start(s32[2,4,16]{2,1,0:T(4,128)S(1)} %get-tuple-element.2527), channel_id=1, source_target_pairs={{0,1},{1,2},{2,3},{3,4},{4,5},{5,6},{6,7},{7,8},{8,9},{9,10},{10,1... | collective-permute-start | bytes 1544 | tf_op jit(solution)/shard_map/ppermute | solution.py:26
  12.9 22.5 %collective-permute-start.9 = (s32[2,4,16]{2,1,0:T(4,128)S(1)}, s32[2,4,16]{2,1,0:T(4,128)S(1)}, u32[]{:S(2)}, u32[]{:S(2)}) collective-permute-start(s32[2,4,16]{2,1,0:T(4,128)S(1)} %get-tuple-element.2528), channel_id=1, source_target_pairs={{1,0},{2,1},{3,2},{4,3},{5,4},{6,5},{7,6},{8,7},{9,8},{10,9},{11,1... | collective-permute-start | bytes 1544 | tf_op jit(solution)/shard_map/ppermute | solution.py:27
  38.2 38.0 %copy-start.9 = (bf16[1,1024,512]{2,1,0:T(8,128)(2,1)S(1)}, bf16[1,1024,512]{2,1,0:T(8,128)(2,1)}, u32[]{:S(2)}) copy-start(bf16[1,1024,512]{2,1,0:T(8,128)(2,1)} %all-gather.3.cloned.1.call-done) | copy-start | bytes 3145732
  82.4 16.3 %copy-start.31 = (bf16[2,8,16,512]{3,2,1,0:T(8,128)(2,1)S(1)}, bf16[2,8,16,512]{3,2,1,0:T(8,128)(2,1)}, u32[]{:S(2)}) copy-start(bf16[2,8,16,512]{3,2,1,0:T(8,128)(2,1)} %get-tuple-element.3160) | copy-start | bytes 786436 | tf_op jit(solution)/shard_map/while
  83.2 18.0 %collective-permute-start = (bf16[4,16,1024]{2,1,0:T(8,128)(2,1)}, bf16[4,16,1024]{2,1,0:T(8,128)(2,1)}, u32[]{:S(2)}, u32[]{:S(2)}) collective-permute-start(bf16[4,16,1024]{2,1,0:T(8,128)(2,1)} %get-tuple-element.2975), channel_id=1, source_target_pairs={{1,0},{2,1},{3,2},{4,3},{5,4},{6,5},{7,6},{8,7},{9,8},{10,9},{11,1... | collective-permute-start | bytes 393224 | tf_op jit(solution)/shard_map/while/body/eval_jaxpr/ppermute | solution.py:27
  84.5 16.8 %collective-permute-start.1 = (bf16[4,16,1024]{2,1,0:T(8,128)(2,1)}, bf16[4,16,1024]{2,1,0:T(8,128)(2,1)}, u32[]{:S(2)}, u32[]{:S(2)}) collective-permute-start(bf16[4,16,1024]{2,1,0:T(8,128)(2,1)} %get-tuple-element.2976), channel_id=1, source_target_pairs={{0,1},{1,2},{2,3},{3,4},{4,5},{5,6},{6,7},{7,8},{8,9},{9,10},{10,1... | collective-permute-start | bytes 393224 | tf_op jit(solution)/shard_map/while/body/eval_jaxpr/ppermute | solution.py:26
  140.7 16.3 %copy-start.31 = (bf16[2,8,16,512]{3,2,1,0:T(8,128)(2,1)S(1)}, bf16[2,8,16,512]{3,2,1,0:T(8,128)(2,1)}, u32[]{:S(2)}) copy-start(bf16[2,8,16,512]{3,2,1,0:T(8,128)(2,1)} %get-tuple-element.3160) | copy-start | bytes 786436 | tf_op jit(solution)/shard_map/while
  141.5 18.0 %collective-permute-start = (bf16[4,16,1024]{2,1,0:T(8,128)(2,1)}, bf16[4,16,1024]{2,1,0:T(8,128)(2,1)}, u32[]{:S(2)}, u32[]{:S(2)}) collective-permute-start(bf16[4,16,1024]{2,1,0:T(8,128)(2,1)} %get-tuple-element.2975), channel_id=1, source_target_pairs={{1,0},{2,1},{3,2},{4,3},{5,4},{6,5},{7,6},{8,7},{9,8},{10,9},{11,1... | collective-permute-start | bytes 393224 | tf_op jit(solution)/shard_map/while/body/eval_jaxpr/ppermute | solution.py:27
  142.7 16.8 %collective-permute-start.1 = (bf16[4,16,1024]{2,1,0:T(8,128)(2,1)}, bf16[4,16,1024]{2,1,0:T(8,128)(2,1)}, u32[]{:S(2)}, u32[]{:S(2)}) collective-permute-start(bf16[4,16,1024]{2,1,0:T(8,128)(2,1)} %get-tuple-element.2976), channel_id=1, source_target_pairs={{0,1},{1,2},{2,3},{3,4},{4,5},{5,6},{6,7},{7,8},{8,9},{9,10},{10,1... | collective-permute-start | bytes 393224 | tf_op jit(solution)/shard_map/while/body/eval_jaxpr/ppermute | solution.py:26
  192.8 1.9 collective-permute-start.10
  197.9 17.1 %collective-permute-start.2 = (bf16[4,16,1024]{2,1,0:T(8,128)(2,1)}, bf16[4,16,1024]{2,1,0:T(8,128)(2,1)}, u32[]{:S(2)}, u32[]{:S(2)}) collective-permute-start(bf16[4,16,1024]{2,1,0:T(8,128)(2,1)} %get-tuple-element.3006), channel_id=1, source_target_pairs={{1,0},{2,1},{3,2},{4,3},{5,4},{6,5},{7,6},{8,7},{9,8},{10,9},{11,1... | collective-permute-start | bytes 393224 | tf_op jit(solution)/shard_map/while/body/eval_jaxpr/ppermute | solution.py:27
  199.2 15.8 %collective-permute-start.3 = (bf16[4,16,1024]{2,1,0:T(8,128)(2,1)}, bf16[4,16,1024]{2,1,0:T(8,128)(2,1)}, u32[]{:S(2)}, u32[]{:S(2)}) collective-permute-start(bf16[4,16,1024]{2,1,0:T(8,128)(2,1)} %get-tuple-element.3007), channel_id=1, source_target_pairs={{0,1},{1,2},{2,3},{3,4},{4,5},{5,6},{6,7},{7,8},{8,9},{9,10},{10,1... | collective-permute-start | bytes 393224 | tf_op jit(solution)/shard_map/while/body/eval_jaxpr/ppermute | solution.py:26
  225.3 17.1 %collective-permute-start.2 = (bf16[4,16,1024]{2,1,0:T(8,128)(2,1)}, bf16[4,16,1024]{2,1,0:T(8,128)(2,1)}, u32[]{:S(2)}, u32[]{:S(2)}) collective-permute-start(bf16[4,16,1024]{2,1,0:T(8,128)(2,1)} %get-tuple-element.3006), channel_id=1, source_target_pairs={{1,0},{2,1},{3,2},{4,3},{5,4},{6,5},{7,6},{8,7},{9,8},{10,9},{11,1... | collective-permute-start | bytes 393224 | tf_op jit(solution)/shard_map/while/body/eval_jaxpr/ppermute | solution.py:27
  226.6 15.8 %collective-permute-start.3 = (bf16[4,16,1024]{2,1,0:T(8,128)(2,1)}, bf16[4,16,1024]{2,1,0:T(8,128)(2,1)}, u32[]{:S(2)}, u32[]{:S(2)}) collective-permute-start(bf16[4,16,1024]{2,1,0:T(8,128)(2,1)} %get-tuple-element.3007), channel_id=1, source_target_pairs={{0,1},{1,2},{2,3},{3,4},{4,5},{5,6},{6,7},{7,8},{8,9},{9,10},{10,1... | collective-permute-start | bytes 393224 | tf_op jit(solution)/shard_map/while/body/eval_jaxpr/ppermute | solution.py:26
  255.1 11.4 %collective-permute-start.6 = (bf16[4,16,1024]{2,1,0:T(8,128)(2,1)}, bf16[4,16,1024]{2,1,0:T(8,128)(2,1)}, u32[]{:S(2)}, u32[]{:S(2)}) collective-permute-start(bf16[4,16,1024]{2,1,0:T(8,128)(2,1)} %get-tuple-element.3072), channel_id=1, source_target_pairs={{0,1},{1,2},{2,3},{3,4},{4,5},{5,6},{6,7},{7,8},{8,9},{9,10},{10,1... | collective-permute-start | bytes 393224 | tf_op jit(solution)/shard_map/while/body/eval_jaxpr/ppermute | solution.py:26
  259.4 8.4 collective-permute-start.7
  284.2 14.1 %collective-permute-start.6 = (bf16[4,16,1024]{2,1,0:T(8,128)(2,1)}, bf16[4,16,1024]{2,1,0:T(8,128)(2,1)}, u32[]{:S(2)}, u32[]{:S(2)}) collective-permute-start(bf16[4,16,1024]{2,1,0:T(8,128)(2,1)} %get-tuple-element.3072), channel_id=1, source_target_pairs={{0,1},{1,2},{2,3},{3,4},{4,5},{5,6},{6,7},{7,8},{8,9},{9,10},{10,1... | collective-permute-start | bytes 393224 | tf_op jit(solution)/shard_map/while/body/eval_jaxpr/ppermute | solution.py:26
  290.9 7.4 collective-permute-start.7
  310.9 144.9 %collective-permute-start.11 = (bf16[2,8,16,512]{3,2,1,0:T(8,128)(2,1)}, bf16[2,8,16,512]{3,2,1,0:T(8,128)(2,1)S(1)}, u32[]{:S(2)}, u32[]{:S(2)}) collective-permute-start(bf16[2,8,16,512]{3,2,1,0:T(8,128)(2,1)} %get-tuple-element.2101), channel_id=1, source_target_pairs={{0,32},{32,0},{1,33},{33,1},{2,34},{34,2},{3,35},{35,3},{4,36},{36... | collective-permute-start | bytes 786440 | tf_op jit(solution)/shard_map/ppermute | solution.py:33
  456.6 43.5 %copy-start.10 = (f32[512,512]{1,0:T(8,128)S(1)}, f32[512,512]{1,0:T(8,128)}, u32[]{:S(2)}) copy-start(f32[512,512]{1,0:T(8,128)} %get-tuple-element.3359) | copy-start | bytes 3145732 | tf_op jit(solution)/shard_map/while
  492.6 10.3 %collective-permute-start.4 = (bf16[4,16,1024]{2,1,0:T(8,128)(2,1)S(1)}, bf16[4,16,1024]{2,1,0:T(8,128)(2,1)}, u32[]{:S(2)}, u32[]{:S(2)}) collective-permute-start(bf16[4,16,1024]{2,1,0:T(8,128)(2,1)S(1)} %get-tuple-element.3040), channel_id=1, source_target_pairs={{0,1},{1,2},{2,3},{3,4},{4,5},{5,6},{6,7},{7,8},{8,9},{9,10},{10,1... | collective-permute-start | bytes 393224 | tf_op jit(solution)/shard_map/while/body/eval_jaxpr/ppermute | solution.py:26
  498.8 7.0 collective-permute-start.5
  522.9 41.3 %copy-start.10 = (f32[512,512]{1,0:T(8,128)S(1)}, f32[512,512]{1,0:T(8,128)}, u32[]{:S(2)}) copy-start(f32[512,512]{1,0:T(8,128)} %get-tuple-element.3359) | copy-start | bytes 3145732 | tf_op jit(solution)/shard_map/while
  558.9 8.2 collective-permute-start.4
  562.9 8.1 collective-permute-start.5
  589.5 62.9 %reduce-scatter.7.cloned.1.call-start = ((), (), s32[]{:S(2)}) async-start(), calls=%async_computation.6 | async-start | bytes 1310720 | tf_op jit(solution)/shard_map/reduce_scatter | solution.py:327
  592.4 91.3 %reduce-scatter.9.cloned.1.call-start = ((), (), s32[]{:S(2)}) async-start(), calls=%async_computation.7 | async-start | bytes 1966080 | tf_op jit(solution)/shard_map/reduce_scatter | solution.py:330
  595.7 113.3 %reduce-scatter.13.cloned.1.call-start = ((), (), s32[]{:S(2)}) async-start(), calls=%async_computation.9 | async-start | bytes 163840
  596.5 266.7 %all-reduce.11.cloned.1.call-start = ((), (), s32[]{:S(2)}) async-start(), calls=%async_computation.10 | async-start | bytes 1572864 | tf_op jit(solution)/shard_map/psum | solution.py:341
  (64 other events, 277.0 us)
Sparse Core Ops, SparseCore 0:
  9.8 28.3 all-gather.2
  40.0 30.3 all-gather.4
  589.7 34.3 reduce-scatter.10
  626.5 25.9 reduce-scatter.6
  655.0 28.5 reduce-scatter.8
  686.7 22.2 reduce-scatter.12
  712.6 150.6 all-reduce.10
where the time goes:
time: 888 us; the launch traced here: 876 us
  waiting for transfers between devices  237 us (27%)
  starting transfers between devices  201 us (23%)
  local copies, waits for them, and re-layouts  166 us (19%)
  other arithmetic  116 us (13%)
  blocking collectives  96.5 us (11%)
  matrix products  42.6 us (5%)
  between operations  14.6 us (2%)
    ppermute x2, starting transfers between devices, partner(): lax.ppermute(shard, axis, [(i, i ^ 1 << distance) for i in range(lax.axis...  144 us
    psum x1, waiting for transfers between devices, body(): lax.psum(merge_part_sum.astype(jnp.bfloat16), 'band').astype(jnp.float32)  77.6 us
    psum x1, blocking collectives, body(): lax.psum(gain_part_sum.astype(jnp.bfloat16), 'band').astype(jnp.float32)  75.3 us
    ppermute x9, starting transfers between devices, padded(): before = lax.ppermute(last, axis, up)  45.6 us
    slice x20, local copies, waits for them, and re-layouts, attend(): key_pairs = jnp.concatenate([kv_blocks[:-1], kv_blocks[1:]], axis=1)  38.4 us
    all_gather x1, waiting for transfers between devices, body(): lax.all_gather(qkv_weight, 'dp', axis=1, tiled=True)  32.2 us
    reduce_scatter x1, waiting for transfers between devices, body(): lax.psum_scatter(grad_sums[1][None].astype(jnp.bfloat16), 'dp', scatter_d...  31.1 us
    dynamic_update_slice x26, other arithmetic, place_one(): lax.dynamic_update_index_in_dim(buffer, jnp.where(active, new_value, curr...  30.9 us
  transfers between devices with their start and end apart: 27, of which 12 were waited for; matrix products, arithmetic and copies ran while one was open for 8% of the time, Pallas kernels for 0%

commit v1 on v0

v1 whole, which is shorter than its diff:
```python
import functools

import jax
import jax.numpy as jnp
from jax import lax
from jax.experimental import pallas as pl
from jax.experimental.pallas import tpu as pltpu
from jax.sharding import PartitionSpec as P

D = 512
HEADS = 8
NX = 4
NY = 4
NZ = 8
TOK = 128
HALF = 64
COLS = 5 * D
EPSILON = 1e-05
MASKED = -1e30
SWAP = (0, 2, 1, 3)
VMEM_LIMIT = 56 * 1024 * 1024
MESH = pl.DeviceIdType.MESH
BF = jnp.bfloat16
F32 = jnp.float32


def dot(left, right):
    return lax.dot_general(left, right, (((1,), (0,)), ((), ())), preferred_element_type=F32)


def dot_nt(left, right):
    return lax.dot_general(left, right, (((1,), (1,)), ((), ())), preferred_element_type=F32)


def dot_tn(left, right):
    return lax.dot_general(left, right, (((0,), (0,)), ((), ())), preferred_element_type=F32)


def rows(index, size):
    return pl.ds(pl.multiple_of(index * size, size), size)


class Links:
    def __init__(self, send, recv, local):
        self.send, self.recv, self.local = send, recv, local
        self.used = 0
        self.used_local = 0
        self.started = []

    def put(self, src, dst, device):
        copy = pltpu.make_async_remote_copy(
            src_ref=src,
            dst_ref=dst,
            send_sem=self.send.at[self.used],
            recv_sem=self.recv.at[self.used],
            device_id=device,
            device_id_type=MESH,
        )
        self.used += 1
        self.started.append(copy)
        copy.start()
        return copy

    def keep(self, src, dst):
        copy = pltpu.make_async_copy(src, dst, self.local.at[self.used_local])
        self.used_local += 1
        copy.start()
        return copy

    def drain(self):
        for copy in self.started:
            copy.wait_send()


def place():
    d = lax.axis_index("dp")
    s = lax.axis_index("segment")
    b = lax.axis_index("band")
    return d, s, b


def x_dev(d, step):
    return {"dp": lax.rem(d + step, NX)}


def y_dev(b, step):
    z, y = b // NY, lax.rem(b, NY)
    return {"band": z * NY + lax.rem(y + step, NY)}


def z_dev(b, step):
    z, y = b // NY, lax.rem(b, NY)
    return {"band": lax.rem(z + step, NZ) * NY + y}


def barrier(devices):
    sem = pltpu.get_barrier_semaphore()
    for device in devices:
        pl.semaphore_signal(sem, inc=1, device_id=device, device_id_type=MESH)
    pl.semaphore_wait(sem, len(devices))


def band_step(b, step):
    count = NY * NZ
    return lax.rem(b + step + count, count)


def gather_kernel(x_in, g_in, use_in, wm_in, wq_in, wo_in, gain_in,
                  x_out, g_out, use_out, wm, wq, wo, gain, send, recv, local):
    d, s, b = place()
    right, left = x_dev(d, 1), x_dev(d, NX - 1)
    core = {"segment": 1 - s}
    before, after = {"band": band_step(b, -1)}, {"band": band_step(b, 1)}
    barrier([right, left, core, before, after])
    link = Links(send, recv, local)
    shifted = [
        link.put(x_in.at[s, pl.ds(0, HALF)], x_out.at[pl.ds(HALF, HALF)], before),
        link.put(use_in, use_out.at[1], before),
        link.put(g_in.at[s, pl.ds(0, HALF)], g_out.at[pl.ds(HALF, HALF)], before),
    ]
    own = [
        link.keep(x_in.at[s, pl.ds(HALF, HALF)], x_out.at[pl.ds(0, HALF)]),
        link.keep(use_in, use_out.at[0]),
        link.keep(g_in.at[s, pl.ds(HALF, HALF)], g_out.at[pl.ds(0, HALF)]),
    ]
    parts = ((wm_in, wm, 2 * TOK), (wq_in, wq, TOK), (wo_in, wo, TOK))

    def full(buffer, owner, size):
        return buffer.at[s, rows(owner, size)]

    def half(buffer, owner, size, which):
        start = pl.multiple_of(owner * size + which * (size // 2), size // 2)
        return buffer.at[s, pl.ds(start, size // 2)]

    to_right, to_left, to_core = [], [], []
    for src, dst, size in parts:
        to_right.append(link.put(src.at[0], full(dst, d, size), right))
        to_left.append(link.put(src.at[0], full(dst, d, size), left))
    gain_right = link.put(gain_in, gain.at[s, d], right)
    gain_left = link.put(gain_in, gain.at[s, d], left)
    for src, dst, size in parts:
        to_core.append(link.put(src.at[0], full(dst, d, size), core))
        own.append(link.keep(src.at[0], full(dst, d, size)))
    to_core.append(link.put(gain_in, gain.at[s, d], core))
    own.append(link.keep(gain_in, gain.at[s, d]))
    from_left, from_right = lax.rem(d + NX - 1, NX), lax.rem(d + 1, NX)
    across = lax.rem(d + 2, NX)
    far = []
    for index, (src, dst, size) in enumerate(parts):
        to_right[index].wait_recv()
        one = link.put(half(dst, from_left, size, 0), half(dst, from_left, size, 0), right)
        to_core.append(link.put(full(dst, from_left, size), full(dst, from_left, size), core))
        to_left[index].wait_recv()
        two = link.put(half(dst, from_right, size, 1), half(dst, from_right, size, 1), left)
        to_core.append(link.put(full(dst, from_right, size), full(dst, from_right, size), core))
        far.append((one, two))
    gain_right.wait_recv()
    gain_far = link.put(gain.at[s, from_left], gain.at[s, from_left], right)
    to_core.append(link.put(gain.at[s, from_left], gain.at[s, from_left], core))
    gain_left.wait_recv()
    to_core.append(link.put(gain.at[s, from_right], gain.at[s, from_right], core))
    for index, (src, dst, size) in enumerate(parts):
        one, two = far[index]
        one.wait_recv()
        two.wait_recv()
        to_core.append(link.put(full(dst, across, size), full(dst, across, size), core))
    gain_far.wait_recv()
    to_core.append(link.put(gain.at[s, across], gain.at[s, across], core))
    for copy in shifted + to_core:
        copy.wait_recv()
    for copy in own:
        copy.wait()
    link.drain()


def compute_kernel(x_ref, cot_ref, use_ref, wm, wq, wo, gain, y_ref, grads, gain_grads,
                   normed_ref, hidden_ref, proj_ref, prob_ref, mix_ref, dproj_ref):
    b = lax.axis_index("band")
    last = b == lax.axis_size("band") - 1
    lane = lax.broadcasted_iota(jnp.int32, (8, TOK), 1)
    own_use = pltpu.roll(use_ref[0], HALF, 1)
    next_use = pltpu.roll(use_ref[1], HALF, 1)
    usable = jnp.where(lane < HALF, own_use, next_use)[0:1]
    query = lax.broadcasted_iota(jnp.int32, (TOK, TOK), 0)
    key = lax.broadcasted_iota(jnp.int32, (TOK, TOK), 1)
    same_lon = (query % 16 // 8) == (key % 16 // 8)
    same_lat = ((query // HALF) == (key // HALF)) | jnp.logical_not(last)
    open_key = jnp.broadcast_to(usable, (TOK, TOK)) > 0.5
    allowed = same_lon & same_lat & (open_key | (query == key))
    first = lax.broadcasted_iota(jnp.int32, (TOK, TOK), 1) < HALF
    zero = jnp.zeros((TOK, TOK), F32)
    head0 = jnp.where(first, zero + 1.0, zero).astype(BF)
    head1 = jnp.where(first, zero, zero + 1.0).astype(BF)

    def pair_cat(values):
        return jnp.concatenate([values * head0, values * head1], axis=0)

    def gain_row(sec):
        return jnp.concatenate([gain[sec, j][0:1] for j in range(4)], axis=1)

    def forward(sec, x):
        update = dot(x, wm[sec, 0:D]) + dot(x, wm[sec, D : 2 * D])
        average = jnp.mean(update, axis=-1, keepdims=True)
        centered = update - average
        spread = jnp.mean(centered * centered, axis=-1, keepdims=True)
        inverse = lax.rsqrt(spread + EPSILON)
        normed = centered * inverse
        normed_ref[sec] = normed
        hidden = (normed * gain_row(sec)).astype(BF)
        hidden_ref[sec] = hidden
        proj_ref[sec] = dot(hidden, wq[sec]).astype(BF)
        for i in range(HEADS // 2):
            cols = slice(TOK * i, TOK * (i + 1))
            q = proj_ref[sec, :, cols]
            k = proj_ref[sec, :, D + TOK * i : D + TOK * (i + 1)]
            v = proj_ref[sec, :, 2 * D + TOK * i : 2 * D + TOK * (i + 1)]
            scores = dot_nt(q, pair_cat(k)) * 0.125
            probs = []
            for h in range(2):
                one = jnp.where(allowed, scores[:, TOK * h : TOK * (h + 1)], MASKED)
                weights = jnp.exp(one - jnp.max(one, axis=-1, keepdims=True))
                probs.append(weights / jnp.sum(weights, axis=-1, keepdims=True))
            prob = jnp.concatenate(probs, axis=1).astype(BF)
            prob_ref[sec, i] = prob
            mix_ref[sec, :, cols] = dot(prob, pair_cat(v)).astype(BF)
        y = (update + dot(mix_ref[sec], wo[sec])).astype(BF)
        y_ref[sec] = y
        return y, inverse

    def backward(sec, x, g, inverse):
        gm = dot_nt(g, wo[sec]).astype(BF)
        for i in range(HEADS // 2):
            cols = slice(TOK * i, TOK * (i + 1))
            q = proj_ref[sec, :, cols]
            k = proj_ref[sec, :, D + TOK * i : D + TOK * (i + 1)]
            v = proj_ref[sec, :, 2 * D + TOK * i : 2 * D + TOK * (i + 1)]
            gm_pair = gm[:, cols]
            prob = prob_ref[sec, i]
            dprob = dot_nt(gm_pair, pair_cat(v))
            pieces = []
            for h in range(2):
                half = slice(TOK * h, TOK * (h + 1))
                p = prob[:, half].astype(F32)
                dp = dprob[:, half]
                pieces.append(p * (dp - jnp.sum(dp * p, axis=-1, keepdims=True)) * 0.125)
            dscore = jnp.concatenate(pieces, axis=1).astype(BF)
            dproj_ref[:, cols] = dot(dscore, pair_cat(k)).astype(BF)
            dk = dot_tn(dscore, q)
            dv = dot_tn(prob, gm_pair)
            dproj_ref[:, D + TOK * i : D + TOK * (i + 1)] = jnp.where(first, dk[:TOK], dk[TOK:]).astype(BF)
            dproj_ref[:, 2 * D + TOK * i : 2 * D + TOK * (i + 1)] = jnp.where(first, dv[:TOK], dv[TOK:]).astype(BF)
        dhidden = dot_nt(dproj_ref[...], wq[sec])
        normed = normed_ref[sec]
        dgain = jnp.sum(dhidden * normed, axis=0, keepdims=True)
        for j in range(4):
            gain_grads[sec, j] = jnp.broadcast_to(dgain[:, TOK * j : TOK * (j + 1)], (8, TOK))
        dnormed = dhidden * gain_row(sec)
        gu = (
            g.astype(F32)
            + inverse
            * (
                dnormed
                - jnp.mean(dnormed, axis=-1, keepdims=True)
                - normed * jnp.mean(dnormed * normed, axis=-1, keepdims=True)
            )
        ).astype(BF)
        for c in range(4):
            part = slice(TOK * c, TOK * (c + 1))
            swapped = slice(TOK * SWAP[c], TOK * (SWAP[c] + 1))
            grads[sec, swapped, 0:D] = dot_tn(x[:, part], gu).astype(BF)
            grads[sec, part, D : 4 * D] = dot_tn(hidden_ref[sec, :, part], dproj_ref[...]).astype(BF)
            grads[sec, part, 4 * D : 5 * D] = dot_tn(mix_ref[sec, :, part], g).astype(BF)
        return gu

    x0 = x_ref[...]
    y0, inverse0 = forward(0, x0)
    y1, inverse1 = forward(1, y0)
    cot = cot_ref[...]
    gu = backward(1, y0, cot, inverse1)
    chain = dot_nt(gu, wm[1, 0:D]).astype(BF).astype(F32)
    side = dot_nt(gu, wm[1, D : 2 * D]).astype(BF).astype(F32)
    backward(0, x0, (chain + side).astype(BF), inverse0)


def reduce_kernel(y_ref, grads, gain_grads, y_home, total, merge_other, gain_total,
                  core_in, x_one, x_two, x_sum, y_one, y_two, y_sum, z_in, z_all,
                  gain_core, gain_sum, gain_x, gain_y, gain_z, send, recv, local):
    d, s, b = place()
    z, y = b // NY, lax.rem(b, NY)
    other = 1 - s
    core = {"segment": other}
    nxt, prev = band_step(b, 1), band_step(b, -1)
    x_right, x_left = x_dev(d, 1), x_dev(d, NX - 1)
    y_right, y_left = y_dev(b, 1), y_dev(b, NY - 1)
    barrier(
        [core]
        + [x_dev(d, k) for k in range(1, NX)]
        + [y_dev(b, k) for k in range(1, NY)]
        + [z_dev(b, k) for k in range(1, NZ)]
        + [{"band": nxt}, {"band": prev}]
        + [{"band": nxt, "segment": other}, {"band": prev, "segment": other}]
    )
    link = Links(send, recv, local)
    lo, hi = pl.ds(0, HALF), pl.ds(HALF, HALF)

    order = [lax.rem(d + k, NX) for k in (2, 1, 3, 0)]
    core_copies = [
        link.put(grads.at[other, rows(j, TOK)], core_in.at[rows(j, TOK)], core) for j in order
    ]
    gain_core_copy = link.put(gain_grads.at[other], gain_core, core)
    home = [
        link.put(y_ref.at[s, hi], y_home.at[s, lo], {"band": nxt}),
        link.put(y_ref.at[other, lo], y_home.at[s, hi], core),
        link.put(y_ref.at[other, hi], y_home.at[s, lo], {"band": nxt, "segment": other}),
    ]
    stays = link.keep(y_ref.at[s, lo], y_home.at[s, hi])

    def add_rows(count, step, terms, store):
        def one(i, carry):
            at = pl.ds(pl.multiple_of(i * step, step), step)
            value = None
            for term in terms:
                loaded = term(at).astype(F32)
                value = loaded if value is None else value + loaded
            store(at, value.astype(BF))
            return carry

        lax.fori_loop(0, count // step, one, 0)

    def at_row(j, at_size):
        return lambda i: None

    def core_sum(which, j):
        core_copies[which].wait_recv()
        base = j * TOK

        def one(i, carry):
            at = pl.ds(pl.multiple_of(base + i * 16, 16), 16)
            grads[s, at] = (grads[s, at].astype(F32) + core_in[at].astype(F32)).astype(BF)
            return carry

        lax.fori_loop(0, TOK // 16, one, 0)

    def chunk_half(j, which):
        return grads.at[s, pl.ds(pl.multiple_of(j * TOK + which * HALF, HALF), HALF)]

    core_sum(0, order[0])
    one_right = link.put(chunk_half(order[0], 0), x_one.at[0], x_right)
    one_left = link.put(chunk_half(order[0], 1), x_one.at[1], x_left)
    gain_core_copy.wait_recv()
    gain_sum[...] = gain_grads[s] + gain_core[...]
    gain_x[0] = gain_sum[d]
    gain_copies = [
        link.put(gain_sum.at[lax.rem(d + k, NX)], gain_x.at[k], x_dev(d, k)) for k in range(1, NX)
    ]
    core_sum(1, order[1])
    one_right.wait_recv()

    def fold(j, offset, source):
        def one(i, carry):
            at = pl.ds(pl.multiple_of(j * TOK + offset + i * 16, 16), 16)
            src = pl.ds(pl.multiple_of(i * 16, 16), 16)
            grads[s, at] = (grads[s, at].astype(F32) + source[src].astype(F32)).astype(BF)
            return carry

        lax.fori_loop(0, HALF // 16, one, 0)

    fold(order[1], 0, x_one.at[0])
    two_right = link.put(grads.at[s, rows(order[1], TOK)], x_two.at[0], x_right)
    core_sum(2, order[2])
    one_left.wait_recv()
    fold(order[2], HALF, x_one.at[1])
    two_left = link.put(grads.at[s, rows(order[2], TOK)], x_two.at[1], x_left)
    core_sum(3, order[3])
    for copy in gain_copies:
        copy.wait_recv()
    gain_y[0] = gain_x[0] + gain_x[1] + gain_x[2] + gain_x[3]
    gain_copies = [link.put(gain_y.at[0], gain_y.at[k], y_dev(b, k)) for k in range(1, NY)]
    two_right.wait_recv()
    two_left.wait_recv()

    def x_add(i, carry):
        at = pl.ds(pl.multiple_of(i * 16, 16), 16)
        mine = pl.ds(pl.multiple_of(d * TOK + i * 16, 16), 16)
        x_sum[at] = (
            grads[s, mine].astype(F32) + x_two[0, at].astype(F32) + x_two[1, at].astype(F32)
        ).astype(BF)
        return carry

    lax.fori_loop(0, TOK // 16, x_add, 0)

    wide = COLS // NY

    def col(j):
        return pl.ds(pl.multiple_of(j * wide, 128), wide)

    yn = [lax.rem(y + k, NY) for k in range(NY)]
    if NY == 4:
        one_right = link.put(x_sum.at[lo, col(yn[2])], y_one.at[0], y_right)
        one_left = link.put(x_sum.at[hi, col(yn[2])], y_one.at[1], y_left)
        one_right.wait_recv()
        x_sum[lo, col(yn[1])] = (x_sum[lo, col(yn[1])].astype(F32) + y_one[0].astype(F32)).astype(BF)
        two_right = link.put(x_sum.at[:, col(yn[1])], y_two.at[0], y_right)
        one_left.wait_recv()
        x_sum[hi, col(yn[3])] = (x_sum[hi, col(yn[3])].astype(F32) + y_one[1].astype(F32)).astype(BF)
        two_left = link.put(x_sum.at[:, col(yn[3])], y_two.at[1], y_left)
    else:
        two_right = link.put(x_sum.at[:, col(yn[1])], y_two.at[0], y_right)
    for copy in gain_copies:
        copy.wait_recv()
    gain_z[0] = functools.reduce(lambda p, q: p + q, [gain_y[k] for k in range(NY)])
    gain_copies = [link.put(gain_z.at[0], gain_z.at[k], z_dev(b, k)) for k in range(1, NZ)]
    two_right.wait_recv()
    value = x_sum[:, col(y)].astype(F32) + y_two[0].astype(F32)
    if NY == 4:
        two_left.wait_recv()
        value = value + y_two[1].astype(F32)
    y_sum[...] = value.astype(BF)

    tall = TOK // NZ
    z_copies = [
        link.put(y_sum.at[rows(lax.rem(z + k, NZ), tall)], z_in.at[k], z_dev(b, k))
        for k in range(1, NZ)
    ]
    mine = rows(z, tall)
    value = y_sum[mine].astype(F32)
    for k in range(1, NZ):
        z_copies[k - 1].wait_recv()
        value = value + z_in[k].astype(F32)
    z_all[mine] = value.astype(BF)
    z_copies = [link.put(z_all.at[mine], z_all.at[mine], z_dev(b, k)) for k in range(1, NZ)]
    for copy in gain_copies:
        copy.wait_recv()
    gain_total[...] = functools.reduce(lambda p, q: p + q, [gain_z[k] for k in range(NZ)])
    for copy in z_copies:
        copy.wait_recv()

    to_right = link.put(z_all, total.at[:, col(y)], y_right)
    if NY == 4:
        to_left = link.put(z_all, total.at[:, col(y)], y_left)
    total[:, col(y)] = z_all[...]
    to_right.wait_recv()
    if NY == 4:
        far_right = link.put(total.at[lo, col(yn[3])], total.at[lo, col(yn[3])], y_right)
        to_left.wait_recv()
        far_left = link.put(total.at[hi, col(yn[1])], total.at[hi, col(yn[1])], y_left)
        far_right.wait_recv()
        far_left.wait_recv()
    merge_copy = link.put(total.at[:, pl.ds(0, D)], merge_other, x_dev(d, 2))
    merge_copy.wait_recv()
    for copy in home:
        copy.wait_recv()
    stays.wait()
    link.drain()


def vmem(count):
    return [pl.BlockSpec(memory_space=pltpu.VMEM)] * count


def anywhere(count):
    return [pl.BlockSpec(memory_space=pl.ANY)] * count


def shape(dims, dtype=BF):
    return jax.ShapeDtypeStruct(dims, dtype)


def sems(count, local):
    return [
        pltpu.SemaphoreType.DMA((count,)),
        pltpu.SemaphoreType.DMA((count,)),
        pltpu.SemaphoreType.DMA((local,)),
    ]


def params(collective):
    if collective is None:
        return pltpu.CompilerParams(vmem_limit_bytes=VMEM_LIMIT)
    return pltpu.CompilerParams(
        collective_id=collective, has_side_effects=True, vmem_limit_bytes=VMEM_LIMIT
    )


def body(fields, cell_mask, merge_weight, qkv_weight, out_weight, norm_gain, out_cotangent):
    d, s, b = place()
    x_in = fields.reshape(2, TOK, D)
    g_in = out_cotangent.reshape(2, TOK, D)
    mask = lax.dynamic_index_in_dim(cell_mask[0], s, 0, keepdims=False).reshape(1, TOK)
    use = jnp.broadcast_to((mask == 1).astype(F32), (8, TOK))
    gain = jnp.broadcast_to(norm_gain.astype(F32), (8, TOK))
    x, cot, use, wm, wq, wo, gains = pl.pallas_call(
        gather_kernel,
        out_shape=(
            shape((TOK, D)), shape((TOK, D)), shape((2, 8, TOK), F32),
            shape((2, 2 * D, D)), shape((2, D, 3 * D)), shape((2, D, D)),
            shape((2, 4, 8, TOK), F32),
        ),
        in_specs=anywhere(7),
        out_specs=vmem(7),
        scratch_shapes=sems(40, 8),
        compiler_params=params(0),
        name="gather",
    )(x_in, g_in, use, merge_weight, qkv_weight, out_weight, gain)
    y, grads, gain_grads = pl.pallas_call(
        compute_kernel,
        out_shape=(shape((2, TOK, D)), shape((2, D, COLS)), shape((2, 4, 8, TOK), F32)),
        in_specs=vmem(7),
        out_specs=vmem(3),
        scratch_shapes=[
            pltpu.VMEM((2, TOK, D), F32),
            pltpu.VMEM((2, TOK, D), BF),
            pltpu.VMEM((2, TOK, 3 * D), BF),
            pltpu.VMEM((2, HEADS // 2, TOK, 2 * TOK), BF),
            pltpu.VMEM((2, TOK, D), BF),
            pltpu.VMEM((TOK, 3 * D), BF),
        ],
        compiler_params=params(None),
        name="compute",
    )(x, cot, use, wm, wq, wo, gains)
    wide = COLS // NY
    home, total, merge_other, gain_total = pl.pallas_call(
        reduce_kernel,
        out_shape=(
            shape((2, TOK, D)), shape((TOK, COLS)), shape((TOK, D)), shape((8, TOK), F32),
        ),
        in_specs=vmem(3),
        out_specs=vmem(4),
        scratch_shapes=[
            pltpu.VMEM((D, COLS), BF),
            pltpu.VMEM((2, HALF, COLS), BF),
            pltpu.VMEM((2, TOK, COLS), BF),
            pltpu.VMEM((TOK, COLS), BF),
            pltpu.VMEM((2, HALF, wide), BF),
            pltpu.VMEM((2, TOK, wide), BF),
            pltpu.VMEM((TOK, wide), BF),
            pltpu.VMEM((NZ, TOK // NZ, wide), BF),
            pltpu.VMEM((TOK, wide), BF),
            pltpu.VMEM((4, 8, TOK), F32),
            pltpu.VMEM((4, 8, TOK), F32),
            pltpu.VMEM((4, 8, TOK), F32),
            pltpu.VMEM((NY, 8, TOK), F32),
            pltpu.VMEM((NZ, 8, TOK), F32),
        ] + sems(64, 2),
        compiler_params=params(1),
        name="reduce",
    )(y, grads, gain_grads)
    section_home = home.reshape(1, 1, 2, 8, 16, D)
    own_merge, other_merge = total[:, :D].astype(F32), merge_other.astype(F32)
    upper = d // 2 == 1
    merge_grad = jnp.where(
        upper,
        jnp.concatenate([other_merge, own_merge], axis=0),
        jnp.concatenate([own_merge, other_merge], axis=0),
    )[None]
    qkv_grad = total[:, D : 4 * D].astype(F32)[None]
    out_grad = total[:, 4 * D :].astype(F32)[None]
    return (section_home, merge_grad, qkv_grad, out_grad, gain_total[0:1])


def solution(mesh):
    return jax.shard_map(
        body,
        mesh=mesh,
        in_specs=(
            P("dp", None, "band", None, None),
            P("dp", None, "band", None),
            P("segment", "dp", None),
            P("segment", "dp", None),
            P("segment", "dp", None),
            P("segment", "dp"),
            P("dp", None, "band", None, None),
        ),
        out_specs=(
            P("segment", "dp", None, "band", None, None),
            P("segment", "dp", None),
            P("segment", "dp", None),
            P("segment", "dp", None),
            P("segment", "dp"),
        ),
        check_vma=False,
    )
```

time: 888 us -> 135 us (0.15); the launches traced: 876 us -> 134 us
  waiting for transfers between devices: 237 us -> 0 us
  starting transfers between devices: 201 us -> 0 us
  local copies, waits for them, and re-layouts: 166 us -> 3.21 us
  Pallas kernels: 0 us -> 124 us
  other arithmetic: 116 us -> 5.97 us
  blocking collectives: 96.5 us -> 0 us
  matrix products: 42.6 us -> 0 us
  between operations: 14.6 us -> 0.68 us
    ppermute x20 -> x0, starting transfers between devices: 201 us -> none  [the longest x2 144 us: partner(): lax.ppermute(shard, axis, [(i, i ^ 1 << distance) for i in range(lax.axis...]
    pallas_call x0 -> x3, Pallas kernels: none -> 124 us  [the longest x1 69.5 us: body(): pl.pallas_call(reduce_kernel, out_shape=(shape((2, TOK, D)), shape((TOK,...]
    reduce_scatter x3 -> x0, waiting for transfers between devices: 87 us -> none  [the longest x1 31.1 us: body(): lax.psum_scatter(grad_sums[1][None].astype(jnp.bfloat16), 'dp', scatter_d...]
    psum x1 -> x0, waiting for transfers between devices: 77.6 us -> none  [body(): lax.psum(merge_part_sum.astype(jnp.bfloat16), 'band').astype(jnp.float32)]
    psum x1 -> x0, blocking collectives: 75.3 us -> none  [body(): lax.psum(gain_part_sum.astype(jnp.bfloat16), 'band').astype(jnp.float32)]
    slice x45 -> x1, local copies, waits for them, and re-layouts: 60.4 us -> 1.23 us  [body(): return (section_home, merge_grad, qkv_grad, out_grad, gain_total[0:1])]
    dot_general x28 -> x0, matrix products: 36.2 us -> none  [the longest x2 5.61 us: project_back(): jnp.einsum('rwj,rwd->jd', joined, grad_update, preferred_element_type=jnp...]
    all_gather x2 -> x0, waiting for transfers between devices: 34.2 us -> none  [the longest x1 32.2 us: body(): lax.all_gather(qkv_weight, 'dp', axis=1, tiled=True)]
  transfers between devices with their start and end apart: 27 -> 0, of which waited for: 12 -> 0; matrix products, arithmetic and copies ran while one was open for 8% -> 0% of each run, Pallas kernels for 0% -> 0%
where the time goes in v1:
time: 135 us; the launch traced here: 134 us
  Pallas kernels  124 us (92%)
  other arithmetic  5.97 us (4%)
  local copies, waits for them, and re-layouts  3.21 us (2%)
    pallas_call x1, Pallas kernels, body(): pl.pallas_call(reduce_kernel, out_shape=(shape((2, TOK, D)), shape((TOK,...  69.5 us
    pallas_call x1, Pallas kernels, body(): pl.pallas_call(gather_kernel, out_shape=(shape((TOK, D)), shape((TOK, D))...  40.3 us
    pallas_call x1, Pallas kernels, body(): pl.pallas_call(compute_kernel, out_shape=(shape((2, TOK, D)), shape((2, D...  14.3 us

profile of v1, /device:TPU:2, one launch (start us, length us, event | category | flops | bytes accessed | tf_op | source)
XLA Modules:
  0.0 134.1 jit_solution(7512630767890151977)
XLA Ops:
  0.6 0.7 bitcast_convert_fusion.4
  1.3 0.6 broadcast_in_dim.31.gain_in
  1.9 0.7 fusion
  2.6 0.1 reshape.96
  2.7 0.6 broadcast_in_dim.28.use_in
  3.3 40.3 %gather.1 = (bf16[128,512]{1,0:T(8,128)(2,1)}, bf16[128,512]{1,0:T(8,128)(2,1)}, f32[2,8,128]{2,1,0:T(8,128)}, bf16[2,1024,512]{2,1,0:T(8,128)(2,1)}, bf16[2,512...) custom-call(bf16[2,128,512]{2,1,0:T(8,128)(2,1)} %bitcast.20, ...), custom_call_target="tpu_custom_call" | custom-call | tf_op jit(solution)/shard_map/gather/pallas_call | solution.py:492
  43.6 14.3 %compute.1 = (bf16[2,128,512]{2,1,0:T(8,128)(2,1)}, bf16[2,512,2560]{2,1,0:T(8,128)(2,1)}, f32[2,4,8,128]{3,2,1,0:T(8,128)}) custom-call(bf16[128,512]{1,0:T(8,128)(2,1)} %get-tuple-element.19.x_ref, bf16[128,512]{1,0:T(8,128)(2,1)} %get-tuple-element.20.cot_ref, f32[2,8,128]{2,1,0:T(8,128)} %get-tuple-element.21.use_ref, ...), custom_call_target="tpu_custom_call" | custom-call | tf_op jit(solution)/shard_map/compute/pallas_call | solution.py:505
  57.9 69.5 %reduce.1 = (bf16[2,128,512]{2,1,0:T(8,128)(2,1)}, bf16[128,2560]{1,0:T(8,128)(2,1)}, bf16[128,512]{1,0:T(8,128)(2,1)}, f32[8,128]{1,0:T(8,128)}) custom-call(bf16[2,128,512]{2,1,0:T(8,128)(2,1)} %get-tuple-element.26.y_ref, bf16[2,512,2560]{2,1,0:T(8,128)(2,1)} %get-tuple-element.27.grads, f32[2,4,8,128]{3,2,1,0:T(8,128)} %get-tuple-element.28.gain_grads), custom_call_target="tpu_custom_call" | custom-call | tf_op jit(solution)/shard_map/reduce/pallas_call | solution.py:522
  127.5 0.0 copy-start
  127.5 1.2 slice.15
  128.7 2.0 %bitcast_convert_fusion = f32[1,128,1536]{2,1,0:T(8,128)} fusion(bf16[128,2560]{1,0:T(8,128)(2,1)} %get-tuple-element.31), kind=kLoop, calls=%fused_computation.1 | loop fusion | flops 196608 | bytes 1179648 | tf_op jit(solution)/shard_map/broadcast_in_dim | solution.py:556
  130.7 1.8 %bitcast_convert_fusion.1 = (f32[1,128,512]{2,1,0:T(8,128)}, f32[1,128,512]{2,1,0:T(8,128)S(1)}, f32[1,128,512]{2,1,0:T(8,128)S(1)}) fusion(bf16[128,2560]{1,0:T(8,128)(2,1)} %get-tuple-element.31, bf16[128,512]{1,0:T(8,128)(2,1)} %get-tuple-element.30), kind=kLoop, calls=%fused_computation.2 | loop fusion | flops 196608 | bytes 1179648 | tf_op jit(solution)/shard_map/broadcast_in_dim | solution.py:557
  132.5 0.8 maximum_select_fusion
  133.4 0.0 copy-done
  133.4 0.7 copy.13
Async XLA Ops:
  127.5 5.9 %copy-start = (bf16[2,128,512]{2,1,0:T(8,128)(2,1)S(1)}, bf16[2,128,512]{2,1,0:T(8,128)(2,1)}, u32[]{:S(2)}) copy-start(bf16[2,128,512]{2,1,0:T(8,128)(2,1)} %get-tuple-element.29) | copy-start | bytes 786436

commit v2 on v1

v2 whole, which is shorter than its diff:
```python
import jax
import jax.numpy as jnp
from jax import lax
from jax.experimental import pallas as pl
from jax.experimental.pallas import tpu as pltpu
from jax.sharding import PartitionSpec as P

D = 512
HEADS = 8
NX = 4
NY = 4
NZ = 8
TOK = 128
HALF = 64
WIDE = 3 * D
PART = WIDE // NY
TALL = TOK // NZ
EPSILON = 1e-05
MASKED = -1e30
VMEM_LIMIT = 58 * 1024 * 1024
MESH = pl.DeviceIdType.MESH
BF = jnp.bfloat16
F32 = jnp.float32


def dot(left, right):
    return lax.dot_general(left, right, (((1,), (0,)), ((), ())), preferred_element_type=F32)


def dot_nt(left, right):
    return lax.dot_general(left, right, (((1,), (1,)), ((), ())), preferred_element_type=F32)


def dot_tn(left, right):
    return lax.dot_general(left, right, (((0,), (0,)), ((), ())), preferred_element_type=F32)


def span(index, size, unit=None):
    return pl.ds(pl.multiple_of(index, unit or size), size)


class Hop:
    def __init__(self, net, src, dst, device):
        at = net.used
        net.used += 1
        net.hops.append(self)
        self.copy = pltpu.make_async_remote_copy(
            src_ref=src,
            dst_ref=dst,
            send_sem=net.send.at[at],
            recv_sem=net.recv.at[at],
            device_id=device,
            device_id_type=MESH,
        )
        self.start = self.copy.start
        self.landed = self.copy.wait_recv
        self.sent = self.copy.wait_send


class Net:
    def __init__(self, send, recv, local):
        self.send, self.recv, self.local = send, recv, local
        self.used = 0
        self.kept = 0
        self.hops = []

    def hop(self, src, dst, device):
        return Hop(self, src, dst, device)

    def keep(self, src, dst):
        copy = pltpu.make_async_copy(src, dst, self.local.at[self.kept])
        self.kept += 1
        return copy


def start(hops):
    for hop in hops:
        hop.start()


def landed(hops):
    for hop in hops:
        hop.landed()


def add_into(count, dst, terms):
    def one(i, carry):
        at = i * 16
        value = terms[0](at).astype(F32)
        for term in terms[1:]:
            value = value + term(at).astype(F32)
        dst(at, value.astype(BF))
        return carry

    lax.fori_loop(0, count // 16, one, 0)


class Ring:
    def __init__(self, net, buf, rect, me, right, left, one_in, two_in):
        self.buf, self.one_in, self.two_in = buf, one_in, two_in
        step = [lax.rem(me + k, 4) for k in range(4)]
        self.rects = [rect(j) for j in step]
        self.nr = self.rects[0][1]
        far, after, before = self.rects[2], self.rects[1], self.rects[3]
        half = self.nr // 2
        self.one = [
            net.hop(self.view(far, 0, half), one_in.at[0], right),
            net.hop(self.view(far, half, half), one_in.at[1], left),
        ]
        self.two = [
            net.hop(self.view(after, 0, self.nr), two_in.at[0], right),
            net.hop(self.view(before, 0, self.nr), two_in.at[1], left),
        ]

    def index(self, rect, offset, count):
        r0, nr, c0, nc = rect
        first = pl.ds(offset, count) if isinstance(r0, int) else span(r0 + offset, count, 16)
        second = pl.ds(0, nc) if isinstance(c0, int) else span(c0, nc, 128)
        return (first, second)

    def view(self, rect, offset, count):
        return self.buf.at[self.index(rect, offset, count)]

    def rows_of(self, rect, base):
        r0, nr, c0, nc = rect

        def at(i):
            second = pl.ds(0, nc) if isinstance(c0, int) else span(c0, nc, 128)
            return (span(r0 + base + i, 16), second)

        return at

    def fold(self, which):
        self.one[which].landed()
        half = self.nr // 2
        rect, base = (self.rects[1], 0) if which == 0 else (self.rects[3], half)
        at = self.rows_of(rect, base)
        source = self.one_in.at[which]

        def store(i, value):
            self.buf[at(i)] = value

        add_into(half, store, [lambda i: self.buf[at(i)], lambda i: source[span(i, 16)]])
        self.two[which].start()

    def finish(self, dst):
        landed(self.two)
        at = self.rows_of(self.rects[0], 0)

        def store(i, value):
            dst[span(i, 16)] = value

        add_into(
            self.nr,
            store,
            [
                lambda i: self.buf[at(i)],
                lambda i: self.two_in[0, span(i, 16)],
                lambda i: self.two_in[1, span(i, 16)],
            ],
        )


def x_dev(d, step):
    return {"dp": lax.rem(d + step, NX)}


def y_dev(b, step):
    z, y = b // NY, lax.rem(b, NY)
    return {"band": z * NY + lax.rem(y + step, NY)}


def z_dev(b, step):
    z, y = b // NY, lax.rem(b, NY)
    return {"band": lax.rem(z + step, NZ) * NY + y}


def barrier(devices):
    sem = pltpu.get_barrier_semaphore()
    for device in devices:
        pl.semaphore_signal(sem, inc=1, device_id=device, device_id_type=MESH)
    pl.semaphore_wait(sem, len(devices))


def kernel(x_in, g_in, use_in, wm_in, wq_in, wo_in, gain_in,
           y_home, total, gain_total,
           x_ref, cot_ref, use_ref, wm, wq, wo, gain,
           y_ref, normed_ref, hidden_ref, proj_ref, prob_ref, mix_ref, dproj_ref,
           grads, gain_grads, core_in,
           ax_one, ax_two, ay_one, ay_two, qy_one, qy_two, qx_one, qx_two, a_sum, q_sum,
           y_sum, z_in, z_all,
           gain_core, gain_sum, gain_x, gain_y, gain_z, send, recv, local):
    d = lax.axis_index("dp")
    s = lax.axis_index("segment")
    b = lax.axis_index("band")
    z, y = b // NY, lax.rem(b, NY)
    other = 1 - s
    bands = NY * NZ
    nxt, prev = lax.rem(b + 1, bands), lax.rem(b + bands - 1, bands)
    core = {"segment": other}
    x_right, x_left = x_dev(d, 1), x_dev(d, NX - 1)
    y_right, y_left = y_dev(b, 1), y_dev(b, NY - 1)
    net = Net(send, recv, local)
    lo, hi = pl.ds(0, HALF), pl.ds(HALF, HALF)
    xd = [lax.rem(d + k, NX) for k in range(NX)]
    yd = [lax.rem(y + k, NY) for k in range(NY)]

    barrier(
        [core]
        + [x_dev(d, k) for k in range(1, NX)]
        + [y_dev(b, k) for k in range(1, NY)]
        + [z_dev(b, k) for k in range(1, NZ)]
        + [{"band": nxt}, {"band": prev}]
        + [{"band": nxt, "segment": other}, {"band": prev, "segment": other}]
    )

    shift = [
        net.hop(x_in.at[s, lo], x_ref.at[hi], {"band": prev}),
        net.hop(use_in.at[s], use_ref.at[1], {"band": prev}),
        net.hop(g_in.at[s, lo], cot_ref.at[hi], {"band": prev}),
    ]
    own = [
        net.keep(x_in.at[s, hi], x_ref.at[lo]),
        net.keep(use_in.at[s], use_ref.at[0]),
        net.keep(g_in.at[s, hi], cot_ref.at[lo]),
    ]
    gain[s, d] = jnp.broadcast_to(gain_in[...].astype(F32), (8, TOK))
    gain_hops = [net.hop(gain.at[s, d], gain.at[s, d], x_dev(d, k)) for k in range(1, NX)]
    gain_core_hops = [net.hop(gain.at[s, xd[0]], gain.at[s, xd[0]], core)] + [
        net.hop(gain.at[s, xd[NX - k]], gain.at[s, xd[NX - k]], core) for k in range(1, NX)
    ]

    class Gather:
        def __init__(self, src, dst, size):
            wide = dst.shape[-1]
            cols = span(y * (wide // NY), wide // NY)
            half, quarter = size // 2, size // 4

            def block(owner, offset, count):
                return dst.at[s, span(owner * size + offset, count, count)]

            def strip(owner):
                return dst.at[s, span(owner * size + half, half), cols]

            top, bottom = pl.ds(0, half), pl.ds(half, half)
            self.strips = [net.hop(src.at[0, bottom, cols], strip(d), x_dev(d, k)) for k in range(1, NX)]
            self.right = net.hop(src.at[0, top], block(d, 0, half), x_right)
            self.left = net.hop(src.at[0, top], block(d, 0, half), x_left)
            self.mine = net.hop(src.at[0], block(d, 0, size), core)
            self.local = net.keep(src.at[0], block(d, 0, size))
            self.spread = [
                [net.hop(strip(xd[NX - k]), strip(xd[NX - k]), y_dev(b, m)) for m in range(1, NY)]
                for k in range(1, NX)
            ]
            self.far_right = net.hop(block(xd[3], 0, quarter), block(xd[3], 0, quarter), x_right)
            self.far_left = net.hop(block(xd[1], quarter, quarter), block(xd[1], quarter, quarter), x_left)
            self.across = [
                net.hop(block(xd[NX - k], 0, size), block(xd[NX - k], 0, size), core)
                for k in range(1, NX)
            ]

        def begin(self):
            start(self.strips + [self.right, self.left, self.mine])
            self.local.start()

        def relay(self):
            for k in (1, 3, 2):
                self.strips[k - 1].landed()
                start(self.spread[k - 1])
            self.right.landed()
            self.far_right.start()
            self.left.landed()
            self.far_left.start()

        def pass_on(self):
            for k in (1, 3):
                landed(self.spread[k - 1])
                self.across[k - 1].start()
            landed(self.spread[1])
            landed([self.far_right, self.far_left])
            self.across[1].start()

        def ready(self):
            landed([self.mine] + self.across)
            self.local.wait()

    merge = Gather(wm_in, wm, 2 * TOK)
    qkv = Gather(wq_in, wq, TOK)
    outw = Gather(wo_in, wo, TOK)

    mine = grads.at[s]
    theirs = grads.at[other]
    a_order = [xd[k] for k in (2, 1, 3, 0)]
    q_order = [yd[k] for k in (2, 1, 3, 0)]

    def a_rows(j):
        return (0, span(j * TOK, TOK))

    def q_cols(j):
        return (1, pl.ds(0, D), span(j * PART, PART, 128))

    swap_a = [net.hop(theirs.at[a_rows(j)], core_in.at[a_rows(j)], core) for j in a_order]
    swap_q = [net.hop(theirs.at[q_cols(j)], core_in.at[q_cols(j)], core) for j in q_order]
    gain_swap = net.hop(gain_grads.at[other], gain_core, core)
    ring_ax = Ring(net, mine.at[0], lambda j: (j * TOK, TOK, 0, WIDE), d, x_right, x_left, ax_one, ax_two)
    ring_qy = Ring(net, mine.at[1], lambda j: (0, D, j * PART, PART), y, y_right, y_left, qy_one, qy_two)
    ring_ay = Ring(net, a_sum, lambda j: (0, TOK, j * PART, PART), y, y_right, y_left, ay_one, ay_two)
    ring_qx = Ring(net, q_sum, lambda j: (j * TOK, TOK, 0, PART), d, x_right, x_left, qx_one, qx_two)
    gain_x_hops = [net.hop(gain_sum.at[xd[k]], gain_x.at[k], x_dev(d, k)) for k in range(1, NX)]
    gain_y_hops = [net.hop(gain_y.at[0], gain_y.at[k], y_dev(b, k)) for k in range(1, NY)]
    gain_z_hops = [net.hop(gain_z.at[0], gain_z.at[k], z_dev(b, k)) for k in range(1, NZ)]
    z_rows = span(z * TALL, TALL)
    both = pl.ds(0, 2)
    z_hops = [
        net.hop(
            y_sum.at[both, span(lax.rem(z + k, NZ) * TALL, TALL)], z_in.at[k], z_dev(b, k)
        )
        for k in range(1, NZ)
    ]
    z_back = [net.hop(z_all.at[both, z_rows], z_all.at[both, z_rows], z_dev(b, k)) for k in range(1, NZ)]

    def col(j):
        return span(j * PART, PART, 128)

    all_rows = pl.ds(0, TOK)
    last_right = net.hop(z_all, total.at[both, all_rows, col(y)], y_right)
    last_left = net.hop(z_all, total.at[both, all_rows, col(y)], y_left)
    end_right = net.hop(total.at[both, lo, col(yd[3])], total.at[both, lo, col(yd[3])], y_right)
    end_left = net.hop(total.at[both, hi, col(yd[1])], total.at[both, hi, col(yd[1])], y_left)
    home = [
        net.hop(y_ref.at[other, lo], y_home.at[s, hi], core),
        net.hop(y_ref.at[s, hi], y_home.at[s, lo], {"band": nxt}),
        net.hop(y_ref.at[other, hi], y_home.at[s, lo], {"band": nxt, "segment": other}),
    ]
    stays = net.keep(y_ref.at[s, lo], y_home.at[s, hi])

    def a_core(i):
        swap_a[i].landed()
        base = a_order[i] * TOK

        def at(r):
            return (0, span(base + r, 16))

        def store(r, value):
            mine[at(r)] = value

        add_into(TOK, store, [lambda r: mine[at(r)], lambda r: core_in[at(r)]])

    def q_core(i):
        swap_q[i].landed()
        cols = span(q_order[i] * PART, PART, 128)

        def at(r):
            return (1, span(r, 16), cols)

        def store(r, value):
            mine[at(r)] = value

        add_into(D, store, [lambda r: mine[at(r)], lambda r: core_in[at(r)]])

    def swap():
        for hop_a, hop_q in zip(swap_a, swap_q):
            hop_a.start()
            hop_q.start()
        gain_swap.start()

    def stage1():
        a_core(0)
        start(ring_ax.one)
        q_core(0)
        start(ring_qy.one)
        for i in (1, 2):
            a_core(i)
            q_core(i)
        gain_swap.landed()
        gain_sum[...] = gain_grads[s] + gain_core[...]
        gain_x[0] = gain_sum[d]
        start(gain_x_hops)

    def stage2():
        for which in (0, 1):
            ring_ax.fold(which)
            ring_qy.fold(which)
        a_core(3)
        q_core(3)
        landed(gain_x_hops)
        gain_y[0] = (gain_x[0] + gain_x[1]) + (gain_x[2] + gain_x[3])
        start(gain_y_hops)

    def stage3():
        ring_ax.finish(a_sum)
        start(ring_ay.one)
        ring_qy.finish(q_sum)
        start(ring_qx.one)
        landed(gain_y_hops)
        gain_z[0] = (gain_y[0] + gain_y[1]) + (gain_y[2] + gain_y[3])
        start(gain_z_hops)

    def masks():
        lane = lax.broadcasted_iota(jnp.int32, (16, TOK), 1)
        sub = lax.broadcasted_iota(jnp.int32, (16, TOK), 0)
        spread = (lane % 16 == sub).astype(F32).astype(BF)
        lane8 = lax.broadcasted_iota(jnp.int32, (8, TOK), 1) // 16
        sub8 = lax.broadcasted_iota(jnp.int32, (8, TOK), 0)
        here = dot((use_ref[0] == 1).astype(F32).astype(BF), spread)
        there = dot((use_ref[1] == 1).astype(F32).astype(BF), spread)
        usable = jnp.sum(
            jnp.where(lane8 + 4 == sub8, here, 0.0) + jnp.where(lane8 - 4 == sub8, there, 0.0),
            axis=0, keepdims=True,
        )
        query = lax.broadcasted_iota(jnp.int32, (TOK, TOK), 0)
        key = lax.broadcasted_iota(jnp.int32, (TOK, TOK), 1)
        same_lon = (query % 16 // 8) == (key % 16 // 8)
        same_lat = ((query // HALF) == (key // HALF)) | jnp.logical_not(b == bands - 1)
        open_key = jnp.broadcast_to(usable, (TOK, TOK)) > 0.5
        return same_lon & same_lat & (open_key | (query == key))

    first = lax.broadcasted_iota(jnp.int32, (TOK, TOK), 1) < HALF
    zero = jnp.zeros((TOK, TOK), F32)
    head0 = jnp.where(first, zero + 1.0, zero).astype(BF)
    head1 = jnp.where(first, zero, zero + 1.0).astype(BF)

    def pair_cat(values):
        return jnp.concatenate([values * head0, values * head1], axis=0)

    def gain_row(sec):
        return jnp.concatenate([gain[sec, j][0:1] for j in range(4)], axis=1)

    def tile(sec, which, i):
        return proj_ref[sec, :, which * D + TOK * i : which * D + TOK * (i + 1)]

    def forward_merge(sec, x):
        update = dot(x, wm[sec, 0:D]) + dot(x, wm[sec, D : 2 * D])
        average = jnp.mean(update, axis=-1, keepdims=True)
        centered = update - average
        spread = jnp.mean(centered * centered, axis=-1, keepdims=True)
        inverse = lax.rsqrt(spread + EPSILON)
        normed = centered * inverse
        normed_ref[sec] = normed
        hidden_ref[sec] = (normed * gain_row(sec)).astype(BF)
        return update, inverse

    def forward_attend(sec, allowed):
        proj_ref[sec] = dot(hidden_ref[sec], wq[sec]).astype(BF)
        for i in range(HEADS // 2):
            scores = dot_nt(tile(sec, 0, i), pair_cat(tile(sec, 1, i))) * 0.125
            probs = []
            for h in range(2):
                one = jnp.where(allowed, scores[:, TOK * h : TOK * (h + 1)], MASKED)
                weights = jnp.exp(one - jnp.max(one, axis=-1, keepdims=True))
                probs.append(weights / jnp.sum(weights, axis=-1, keepdims=True))
            prob = jnp.concatenate(probs, axis=1).astype(BF)
            prob_ref[sec, i] = prob
            mix_ref[sec, :, TOK * i : TOK * (i + 1)] = dot(prob, pair_cat(tile(sec, 2, i))).astype(BF)

    def forward_out(sec, update):
        result = (update + dot(mix_ref[sec], wo[sec])).astype(BF)
        y_ref[sec] = result
        return result

    def backward_attend(sec, g):
        gm = dot_nt(g, wo[sec]).astype(BF)
        for i in range(HEADS // 2):
            q, k, v = tile(sec, 0, i), tile(sec, 1, i), tile(sec, 2, i)
            gm_pair = gm[:, TOK * i : TOK * (i + 1)]
            prob = prob_ref[sec, i]
            dprob = dot_nt(gm_pair, pair_cat(v))
            pieces = []
            for h in range(2):
                half = slice(TOK * h, TOK * (h + 1))
                p = prob[:, half].astype(F32)
                dp = dprob[:, half]
                pieces.append(p * (dp - jnp.sum(dp * p, axis=-1, keepdims=True)) * 0.125)
            dscore = jnp.concatenate(pieces, axis=1).astype(BF)
            dk = dot_tn(dscore, q)
            dv = dot_tn(prob, gm_pair)
            dproj_ref[:, TOK * i : TOK * (i + 1)] = dot(dscore, pair_cat(k)).astype(BF)
            dproj_ref[:, D + TOK * i : D + TOK * (i + 1)] = jnp.where(first, dk[:TOK], dk[TOK:]).astype(BF)
            dproj_ref[:, 2 * D + TOK * i : 2 * D + TOK * (i + 1)] = jnp.where(first, dv[:TOK], dv[TOK:]).astype(BF)

    def backward_terms(sec, x, g, inverse):
        dhidden = dot_nt(dproj_ref[...], wq[sec])
        normed = normed_ref[sec]
        dgain = jnp.sum(dhidden * normed, axis=0, keepdims=True)
        for j in range(4):
            gain_grads[sec, j] = jnp.broadcast_to(dgain[:, TOK * j : TOK * (j + 1)], (8, TOK))
        dnormed = dhidden * gain_row(sec)
        gu = (
            g.astype(F32)
            + inverse
            * (
                dnormed
                - jnp.mean(dnormed, axis=-1, keepdims=True)
                - normed * jnp.mean(dnormed * normed, axis=-1, keepdims=True)
            )
        ).astype(BF)
        for c in range(4):
            part = slice(TOK * c, TOK * (c + 1))
            grads[sec, 1, part] = dot_tn(hidden_ref[sec, :, part], dproj_ref[...]).astype(BF)
            grads[sec, 0, part, 2 * D : 3 * D] = dot_tn(mix_ref[sec, :, part], g).astype(BF)
            term = dot_tn(x[:, part], gu).astype(BF)
            for j in (c // 2, c // 2 + 2):
                grads[sec, 0, TOK * j : TOK * (j + 1), D * (c % 2) : D * (c % 2 + 1)] = term
        return gu

    start(shift[:2])
    merge.begin()
    start(gain_hops + gain_core_hops[:1])
    for copy in own:
        copy.start()
    qkv.begin()
    outw.begin()
    shift[2].start()
    merge.relay()
    qkv.relay()
    for k in range(1, NX):
        gain_hops[k - 1].landed()
        gain_core_hops[k].start()
    merge.pass_on()
    landed(gain_core_hops)
    landed(shift)
    for copy in own:
        copy.wait()
    allowed = masks()
    x0 = x_ref[...]
    merge.ready()
    update0, inverse0 = forward_merge(0, x0)
    outw.relay()
    qkv.pass_on()
    qkv.ready()
    forward_attend(0, allowed)
    outw.pass_on()
    outw.ready()
    y0 = forward_out(0, update0)
    update1, inverse1 = forward_merge(1, y0)
    forward_attend(1, allowed)
    forward_out(1, update1)
    start(home)
    stays.start()
    cot = cot_ref[...]
    backward_attend(1, cot)
    gu1 = backward_terms(1, y0, cot, inverse1)

    @pl.when(s == 0)
    def _():
        swap()

    chain = dot_nt(gu1, wm[1, 0:D]).astype(BF).astype(F32)
    side = dot_nt(gu1, wm[1, D : 2 * D]).astype(BF).astype(F32)
    g0 = (chain + side).astype(BF)

    @pl.when(s == 1)
    def _():
        stage1()

    backward_attend(0, g0)

    @pl.when(s == 1)
    def _():
        stage2()

    backward_terms(0, x0, g0, inverse0)

    @pl.when(s == 1)
    def _():
        swap()
        stage3()

    @pl.when(s == 0)
    def _():
        stage1()
        stage2()
        stage3()

    for which in (0, 1):
        ring_ay.fold(which)
        ring_qx.fold(which)
    ring_ay.finish(y_sum.at[0])
    ring_qx.finish(y_sum.at[1])
    start(z_hops)
    value = y_sum[both, z_rows].astype(F32)
    for k in range(1, NZ):
        z_hops[k - 1].landed()
        value = value + z_in[k].astype(F32)
    z_all[both, z_rows] = value.astype(BF)
    start(z_back)
    landed(gain_z_hops)
    gain_value = gain_z[0]
    for k in range(1, NZ):
        gain_value = gain_value + gain_z[k]
    gain_total[...] = gain_value
    landed(z_back)
    start([last_right, last_left])
    total[both, all_rows, col(y)] = z_all[...]
    last_right.landed()
    end_right.start()
    last_left.landed()
    end_left.start()
    landed(home)
    stays.wait()
    landed([end_right, end_left])
    for hop in net.hops:
        hop.sent()


def vmem(count):
    return [pl.BlockSpec(memory_space=pltpu.VMEM)] * count


def anywhere(count):
    return [pl.BlockSpec(memory_space=pl.ANY)] * count


def shape(dims, dtype=BF):
    return jax.ShapeDtypeStruct(dims, dtype)


def body(fields, cell_mask, merge_weight, qkv_weight, out_weight, norm_gain, out_cotangent):
    x_in = fields.reshape(2, TOK, D)
    g_in = out_cotangent.reshape(2, TOK, D)
    use = cell_mask.reshape(2, 8, 16)
    home, total, gain_total = pl.pallas_call(
        kernel,
        out_shape=(shape((2, TOK, D)), shape((2, TOK, WIDE)), shape((8, TOK), F32)),
        in_specs=anywhere(6) + vmem(1),
        out_specs=vmem(3),
        scratch_shapes=[
            pltpu.VMEM((TOK, D), BF),
            pltpu.VMEM((TOK, D), BF),
            pltpu.VMEM((2, 8, 16), jnp.int32),
            pltpu.VMEM((2, 2 * D, D), BF),
            pltpu.VMEM((2, D, 3 * D), BF),
            pltpu.VMEM((2, D, D), BF),
            pltpu.VMEM((2, 4, 8, TOK), F32),
            pltpu.VMEM((2, TOK, D), BF),
            pltpu.VMEM((2, TOK, D), F32),
            pltpu.VMEM((2, TOK, D), BF),
            pltpu.VMEM((2, TOK, 3 * D), BF),
            pltpu.VMEM((2, HEADS // 2, TOK, 2 * TOK), BF),
            pltpu.VMEM((2, TOK, D), BF),
            pltpu.VMEM((TOK, 3 * D), BF),
            pltpu.VMEM((2, 2, D, WIDE), BF),
            pltpu.VMEM((2, 4, 8, TOK), F32),
            pltpu.VMEM((2, D, WIDE), BF),
            pltpu.VMEM((2, HALF, WIDE), BF),
            pltpu.VMEM((2, TOK, WIDE), BF),
            pltpu.VMEM((2, HALF, PART), BF),
            pltpu.VMEM((2, TOK, PART), BF),
            pltpu.VMEM((2, D // 2, PART), BF),
            pltpu.VMEM((2, D, PART), BF),
            pltpu.VMEM((2, HALF, PART), BF),
            pltpu.VMEM((2, TOK, PART), BF),
            pltpu.VMEM((TOK, WIDE), BF),
            pltpu.VMEM((D, PART), BF),
            pltpu.VMEM((2, TOK, PART), BF),
            pltpu.VMEM((NZ, 2, TALL, PART), BF),
            pltpu.VMEM((2, TOK, PART), BF),
            pltpu.VMEM((4, 8, TOK), F32),
            pltpu.VMEM((4, 8, TOK), F32),
            pltpu.VMEM((4, 8, TOK), F32),
            pltpu.VMEM((NY, 8, TOK), F32),
            pltpu.VMEM((NZ, 8, TOK), F32),
            pltpu.SemaphoreType.DMA((144,)),
            pltpu.SemaphoreType.DMA((144,)),
            pltpu.SemaphoreType.DMA((8,)),
        ],
        compiler_params=pltpu.CompilerParams(
            collective_id=0, has_side_effects=True, vmem_limit_bytes=VMEM_LIMIT
        ),
        name="step",
    )(x_in, g_in, use, merge_weight, qkv_weight, out_weight, norm_gain)
    section_home = home.reshape(1, 1, 2, 8, 16, D)
    merge_grad = jnp.concatenate([total[0, :, :D], total[0, :, D : 2 * D]], axis=0).astype(F32)[None]
    qkv_grad = total[1].astype(F32)[None]
    out_grad = total[0, :, 2 * D :].astype(F32)[None]
    return (section_home, merge_grad, qkv_grad, out_grad, gain_total[0:1])


def solution(mesh):
    return jax.shard_map(
        body,
        mesh=mesh,
        in_specs=(
            P("dp", None, "band", None, None),
            P("dp", None, "band", None),
            P("segment", "dp", None),
            P("segment", "dp", None),
            P("segment", "dp", None),
            P("segment", "dp"),
            P("dp", None, "band", None, None),
        ),
        out_specs=(
            P("segment", "dp", None, "band", None, None),
            P("segment", "dp", None),
            P("segment", "dp", None),
            P("segment", "dp", None),
            P("segment", "dp"),
        ),
        check_vma=False,
    )
```

time: 135 us -> 103 us (0.76)
  Pallas kernels: 124 us -> 95.5 us
  other arithmetic: 5.97 us -> 3.58 us
    pallas_call x3 -> x1, Pallas kernels: 124 us -> 95.5 us  [body(): pl.pallas_call(kernel, out_shape=(shape((2, TOK, D)), shape((2, TOK, WIDE...]
    broadcast_in_dim x3 -> x0, other arithmetic: 4.44 us -> none  [the longest x1 1.95 us: body(): qkv_grad = total[:, D:4 * D].astype(F32)[None]]
    convert_element_type x1 -> x3, other arithmetic: 0.69 us -> 3.58 us  [the longest x1 1.77 us: body(): out_grad = total[0, :, 2 * D:].astype(F32)[None]]
where the time goes in v2:
time: 103 us; the launch traced here: 102 us
  Pallas kernels  95.5 us (93%)
  other arithmetic  3.58 us (3%)
  local copies, waits for them, and re-layouts  2.06 us (2%)
    pallas_call x1, Pallas kernels, body(): pl.pallas_call(kernel, out_shape=(shape((2, TOK, D)), shape((2, TOK, WIDE...  95.5 us

profile of v2, /device:TPU:2, one launch (start us, length us, event | category | flops | bytes accessed | tf_op | source)
XLA Modules:
  0.0 101.8 jit_solution(9278460076767283718)
XLA Ops:
  0.6 95.5 %step.1 = (bf16[2,128,512]{2,1,0:T(8,128)(2,1)}, bf16[2,128,1536]{2,1,0:T(8,128)(2,1)}, f32[8,128]{1,0:T(8,128)}) custom-call(bf16[2,128,512]{2,1,0:T(8,128)(2,1)} %bitcast.4, bf16[2,128,512]{2,1,0:T(8,128)(2,1)} %bitcast.5, s32[2,8,16]{2,1,0:T(8,128)} %bitcast.7, bf16[1,256,512]{2,1,0:T(8,128)(2,1)} %wm_in.1, bf16[1,128,1536]{2,1,0:T(8,128)(2,1)} %wq_in.1, ...), custom_call_target="tpu_custom_call" | custom-call | tf_op jit(solution)/shard_map/step/pallas_call | solution.py:622
  96.2 0.0 copy-start
  96.2 1.3 %slice.19 = f32[1,128]{1,0:T(1,128)} slice(f32[8,128]{1,0:T(8,128)} %get-tuple-element.10), slice={[0:1], [0:128]} | slice | bytes 1024 | tf_op jit(solution)/shard_map/slice | solution.py:676
  97.5 1.8 %slice_convert_fusion.1 = (f32[1,128,512]{2,1,0:T(8,128)}, bf16[1,128,512]{2,1,0:T(8,128)(2,1)S(1)}, bf16[1,128,512]{2,1,0:T(8,128)(2,1)S(1)}) fusion(bf16[2,128,1536]{2,1,0:T(8,128)(2,1)} %get-tuple-element.9), kind=kLoop, calls=%fused_computation.2 | loop fusion | flops 65536 | bytes 917504 | tf_op jit(solution)/shard_map/convert_element_type | solution.py:675
  99.2 0.0 copy-done
  99.2 1.0 slice_convert_fusion
  100.2 0.0 copy-start.1
  100.2 0.9 maximum_convert_fusion
  101.0 0.1 copy-done.1
  101.1 0.7 copy.13
Async XLA Ops:
  96.2 3.0 %copy-start = (bf16[2,128,1536]{2,1,0:T(8,128)(2,1)S(1)}, bf16[2,128,1536]{2,1,0:T(8,128)(2,1)}, u32[]{:S(2)}) copy-start(bf16[2,128,1536]{2,1,0:T(8,128)(2,1)} %get-tuple-element.9) | copy-start | bytes 2359300
  100.2 0.9 copy-start.1

commit v3 on v2

--- a/solution.py
+++ b/solution.py
@@ -161,6 +161,42 @@
         )
 
 
+class Direct:
+    def __init__(self, net, buf, rect, me, peer, came_in):
+        self.buf, self.came_in = buf, came_in
+        self.mine = rect(me)
+        self.hops = [
+            net.hop(buf.at[self.index(rect(lax.rem(me + k, 4)), 0, None)], came_in.at[k - 1], peer(k))
+            for k in range(1, 4)
+        ]
+
+    def index(self, rect, offset, count):
+        r0, nr, c0, nc = rect
+        count = count or nr
+        first = pl.ds(offset, count) if isinstance(r0, int) and isinstance(offset, int) else span(r0 + offset, count, 16)
+        second = pl.ds(0, nc) if isinstance(c0, int) else span(c0, nc, 128)
+        return (first, second)
+
+    def begin(self):
+        for k in (2, 1, 3):
+            self.hops[k - 1].start()
+
+    def finish(self, dst):
+        landed(self.hops)
+
+        def store(i, value):
+            dst[span(i, 16)] = value
+
+        def term(k):
+            return lambda i: self.came_in[k, span(i, 16)]
+
+        add_into(
+            self.mine[1],
+            store,
+            [lambda i: self.buf[self.index(self.mine, i, 16)]] + [term(k) for k in range(3)],
+        )
+
+
 def x_dev(d, step):
     return {"dp": lax.rem(d + step, NX)}
 
@@ -187,8 +223,8 @@
            x_ref, cot_ref, use_ref, wm, wq, wo, gain,
            y_ref, normed_ref, hidden_ref, proj_ref, prob_ref, mix_ref, dproj_ref,
            grads, gain_grads, core_in,
-           ax_one, ax_two, ay_one, ay_two, qy_one, qy_two, qx_one, qx_two, a_sum, q_sum,
-           y_sum, z_in, z_all,
+           ax_one, ax_two, qy_one, qy_two, ay_in, qx_in, a_sum, q_sum,
+           y_sum, z_in,
            gain_core, gain_sum, gain_x, gain_y, gain_z, send, recv, local):
     d = lax.axis_index("dp")
     s = lax.axis_index("segment")
@@ -260,13 +296,15 @@
             ]
 
         def begin(self):
-            start(self.strips + [self.right, self.left, self.mine])
+            start([self.right, self.left, self.mine])
             self.local.start()
 
-        def relay(self):
+        def relay_strips(self):
             for k in (1, 3, 2):
                 self.strips[k - 1].landed()
                 start(self.spread[k - 1])
+
+        def relay(self):
             self.right.landed()
             self.far_right.start()
             self.left.landed()
@@ -304,8 +342,8 @@
     gain_swap = net.hop(gain_grads.at[other], gain_core, core)
     ring_ax = Ring(net, mine.at[0], lambda j: (j * TOK, TOK, 0, WIDE), d, x_right, x_left, ax_one, ax_two)
     ring_qy = Ring(net, mine.at[1], lambda j: (0, D, j * PART, PART), y, y_right, y_left, qy_one, qy_two)
-    ring_ay = Ring(net, a_sum, lambda j: (0, TOK, j * PART, PART), y, y_right, y_left, ay_one, ay_two)
-    ring_qx = Ring(net, q_sum, lambda j: (j * TOK, TOK, 0, PART), d, x_right, x_left, qx_one, qx_two)
+    to_ay = Direct(net, a_sum, lambda j: (0, TOK, j * PART, PART), y, lambda k: y_dev(b, k), ay_in)
+    to_qx = Direct(net, q_sum, lambda j: (j * TOK, TOK, 0, PART), d, lambda k: x_dev(d, k), qx_in)
     gain_x_hops = [net.hop(gain_sum.at[xd[k]], gain_x.at[k], x_dev(d, k)) for k in range(1, NX)]
     gain_y_hops = [net.hop(gain_y.at[0], gain_y.at[k], y_dev(b, k)) for k in range(1, NY)]
     gain_z_hops = [net.hop(gain_z.at[0], gain_z.at[k], z_dev(b, k)) for k in range(1, NZ)]
@@ -317,16 +355,12 @@
         )
         for k in range(1, NZ)
     ]
-    z_back = [net.hop(z_all.at[both, z_rows], z_all.at[both, z_rows], z_dev(b, k)) for k in range(1, NZ)]
-
-    def col(j):
-        return span(j * PART, PART, 128)
-
-    all_rows = pl.ds(0, TOK)
-    last_right = net.hop(z_all, total.at[both, all_rows, col(y)], y_right)
-    last_left = net.hop(z_all, total.at[both, all_rows, col(y)], y_left)
-    end_right = net.hop(total.at[both, lo, col(yd[3])], total.at[both, lo, col(yd[3])], y_right)
-    end_left = net.hop(total.at[both, hi, col(yd[1])], total.at[both, hi, col(yd[1])], y_left)
+    def piece(k):
+        at = (both, span(lax.rem(z + NZ - k, NZ) * TALL, TALL), span(y * PART, PART, 128))
+        return total.at[at]
+
+    z_back = [net.hop(piece(0), piece(0), z_dev(b, k)) for k in range(1, NZ)]
+    y_back = [[net.hop(piece(k), piece(k), y_dev(b, m)) for m in range(1, NY)] for k in range(NZ)]
     home = [
         net.hop(y_ref.at[other, lo], y_home.at[s, hi], core),
         net.hop(y_ref.at[s, hi], y_home.at[s, lo], {"band": nxt}),
@@ -389,9 +423,9 @@
 
     def stage3():
         ring_ax.finish(a_sum)
-        start(ring_ay.one)
+        to_ay.begin()
         ring_qy.finish(q_sum)
-        start(ring_qx.one)
+        to_qx.begin()
         landed(gain_y_hops)
         gain_z[0] = (gain_y[0] + gain_y[1]) + (gain_y[2] + gain_y[3])
         start(gain_z_hops)
@@ -503,6 +537,8 @@
                 grads[sec, 0, TOK * j : TOK * (j + 1), D * (c % 2) : D * (c % 2 + 1)] = term
         return gu
 
+    for part in (merge, qkv, outw):
+        start(part.strips)
     start(shift[:2])
     merge.begin()
     start(gain_hops + gain_core_hops[:1])
@@ -511,6 +547,8 @@
     qkv.begin()
     outw.begin()
     shift[2].start()
+    for part in (merge, qkv, outw):
+        part.relay_strips()
     merge.relay()
     qkv.relay()
     for k in range(1, NX):
@@ -555,15 +593,12 @@
 
     backward_attend(0, g0)
 
-    @pl.when(s == 1)
-    def _():
-        stage2()
-
     backward_terms(0, x0, g0, inverse0)
 
     @pl.when(s == 1)
     def _():
         swap()
+        stage2()
         stage3()
 
     @pl.when(s == 0)
@@ -572,35 +607,40 @@
         stage2()
         stage3()
 
-    for which in (0, 1):
-        ring_ay.fold(which)
-        ring_qx.fold(which)
-    ring_ay.finish(y_sum.at[0])
-    ring_qx.finish(y_sum.at[1])
+    to_ay.finish(y_sum.at[0])
+    to_qx.finish(y_sum.at[1])
     start(z_hops)
     value = y_sum[both, z_rows].astype(F32)
     for k in range(1, NZ):
         z_hops[k - 1].landed()
         value = value + z_in[k].astype(F32)
-    z_all[both, z_rows] = value.astype(BF)
+    total[both, z_rows, span(y * PART, PART, 128)] = value.astype(BF)
     start(z_back)
+    start(y_back[0])
     landed(gain_z_hops)
     gain_value = gain_z[0]
     for k in range(1, NZ):
         gain_value = gain_value + gain_z[k]
     gain_total[...] = gain_value
-    landed(z_back)
-    start([last_right, last_left])
-    total[both, all_rows, col(y)] = z_all[...]
-    last_right.landed()
-    end_right.start()
-    last_left.landed()
-    end_left.start()
+    for k in (1, 7, 2, 6, 3, 5, 4):
+        if k < NZ:
+            z_back[k - 1].landed()
+            start(y_back[k])
     landed(home)
     stays.wait()
-    landed([end_right, end_left])
+    for hops in y_back:
+        landed(hops)
     for hop in net.hops:
         hop.sent()
+
+
+def widen(home_in, total, gain_in, home, merge, qkv, out, gain):
+    home[...] = home_in[...]
+    merge[0:TOK] = total[0, :, 0:D].astype(F32)
+    merge[TOK : 2 * TOK] = total[0, :, D : 2 * D].astype(F32)
+    out[...] = total[0, :, 2 * D : 3 * D].astype(F32)
+    qkv[...] = total[1].astype(F32)
+    gain[...] = gain_in[0:1]
 
 
 def vmem(count):
@@ -644,24 +684,21 @@
             pltpu.VMEM((2, D, WIDE), BF),
             pltpu.VMEM((2, HALF, WIDE), BF),
             pltpu.VMEM((2, TOK, WIDE), BF),
-            pltpu.VMEM((2, HALF, PART), BF),
-            pltpu.VMEM((2, TOK, PART), BF),
             pltpu.VMEM((2, D // 2, PART), BF),
             pltpu.VMEM((2, D, PART), BF),
-            pltpu.VMEM((2, HALF, PART), BF),
-            pltpu.VMEM((2, TOK, PART), BF),
+            pltpu.VMEM((3, TOK, PART), BF),
+            pltpu.VMEM((3, TOK, PART), BF),
             pltpu.VMEM((TOK, WIDE), BF),
             pltpu.VMEM((D, PART), BF),
             pltpu.VMEM((2, TOK, PART), BF),
             pltpu.VMEM((NZ, 2, TALL, PART), BF),
-            pltpu.VMEM((2, TOK, PART), BF),
             pltpu.VMEM((4, 8, TOK), F32),
             pltpu.VMEM((4, 8, TOK), F32),
             pltpu.VMEM((4, 8, TOK), F32),
             pltpu.VMEM((NY, 8, TOK), F32),
             pltpu.VMEM((NZ, 8, TOK), F32),
-            pltpu.SemaphoreType.DMA((144,)),
-            pltpu.SemaphoreType.DMA((144,)),
+            pltpu.SemaphoreType.DMA((176,)),
+            pltpu.SemaphoreType.DMA((176,)),
             pltpu.SemaphoreType.DMA((8,)),
         ],
         compiler_params=pltpu.CompilerParams(
@@ -669,11 +706,19 @@
         ),
         name="step",
     )(x_in, g_in, use, merge_weight, qkv_weight, out_weight, norm_gain)
+    home, merge_grad, qkv_grad, out_grad, gain_grad = pl.pallas_call(
+        widen,
+        out_shape=(
+            shape((2, TOK, D)), shape((2 * TOK, D), F32), shape((TOK, 3 * D), F32),
+            shape((TOK, D), F32), shape((1, TOK), F32),
+        ),
+        in_specs=vmem(3),
+        out_specs=vmem(5),
+        compiler_params=pltpu.CompilerParams(vmem_limit_bytes=16 * 1024 * 1024),
+        name="widen",
+    )(home, total, gain_total)
     section_home = home.reshape(1, 1, 2, 8, 16, D)
-    merge_grad = jnp.concatenate([total[0, :, :D], total[0, :, D : 2 * D]], axis=0).astype(F32)[None]
-    qkv_grad = total[1].astype(F32)[None]
-    out_grad = total[0, :, 2 * D :].astype(F32)[None]
-    return (section_home, merge_grad, qkv_grad, out_grad, gain_total[0:1])
+    return (section_home, merge_grad[None], qkv_grad[None], out_grad[None], gain_grad)
 
 
 def solution(mesh):

time: 103 us -> 95.1 us (0.923)
  Pallas kernels: 95.5 us -> 91.3 us
  other arithmetic: 3.58 us -> 0 us
    pallas_call x1, Pallas kernels: 95.5 us -> 89.9 us  [body(): pl.pallas_call(kernel, out_shape=(shape((2, TOK, D)), shape((2, TOK, WIDE...]
    convert_element_type x3 -> x0, other arithmetic: 3.58 us -> none  [the longest x1 1.77 us: body(): out_grad = total[0, :, 2 * D:].astype(F32)[None]]
    unnamed x5 -> x6, local copies, waits for them, and re-layouts: 0.8 us -> 2.76 us
    pallas_call x0 -> x1, Pallas kernels: none -> 1.33 us  [body(): pl.pallas_call(widen, out_shape=(shape((2, TOK, D)), shape((2 * TOK, D),...]
    slice x1 -> x0, local copies, waits for them, and re-layouts: 1.26 us -> none  [body(): return (section_home, merge_grad, qkv_grad, out_grad, gain_total[0:1])]
where the time goes in v3:
time: 95.1 us; the launch traced here: 94.7 us
  Pallas kernels  91.3 us (96%)
  local copies, waits for them, and re-layouts  2.76 us (3%)
    pallas_call x1, Pallas kernels, body(): pl.pallas_call(kernel, out_shape=(shape((2, TOK, D)), shape((2, TOK, WIDE...  89.9 us
    unnamed x6, local copies, waits for them, and re-layouts  2.76 us

profile of v3, /device:TPU:2, one launch (start us, length us, event | category | flops | bytes accessed | tf_op | source)
XLA Modules:
  0.0 94.7 jit_solution(3701862990118378506)
XLA Ops:
  0.6 89.9 %step.1 = (bf16[2,128,512]{2,1,0:T(8,128)(2,1)}, bf16[2,128,1536]{2,1,0:T(8,128)(2,1)}, f32[8,128]{1,0:T(8,128)}) custom-call(bf16[2,128,512]{2,1,0:T(8,128)(2,1)} %bitcast.7, bf16[2,128,512]{2,1,0:T(8,128)(2,1)} %bitcast.8, s32[2,8,16]{2,1,0:T(8,128)} %bitcast.9, bf16[1,256,512]{2,1,0:T(8,128)(2,1)} %wm_in.1, bf16[1,128,1536]{2,1,0:T(8,128)(2,1)} %wq_in.1, ...), custom_call_target="tpu_custom_call" | custom-call | tf_op jit(solution)/shard_map/step/pallas_call | solution.py:662
  90.6 0.0 copy-start.2
  90.6 0.7 copy-done.2
  91.3 0.0 copy-start
  91.3 1.1 %copy-done = bf16[2,128,1536]{2,1,0:T(8,128)(2,1)S(1)} copy-done((bf16[2,128,1536]{2,1,0:T(8,128)(2,1)S(1)}, bf16[2,128,1536]{2,1,0:T(8,128)(2,1)}, u32[]{:S(2)}) %copy-start) | copy-done | bytes 786456
  92.4 0.0 copy-start.1
  92.4 0.9 %copy-done.1 = bf16[2,128,512]{2,1,0:T(8,128)(2,1)S(1)} copy-done((bf16[2,128,512]{2,1,0:T(8,128)(2,1)S(1)}, bf16[2,128,512]{2,1,0:T(8,128)(2,1)}, u32[]{:S(2)}) %copy-start.1) | copy-done | bytes 262168
  93.3 1.3 %widen.1 = (bf16[2,128,512]{2,1,0:T(8,128)(2,1)}, f32[256,512]{1,0:T(8,128)}, f32[128,1536]{1,0:T(8,128)}, f32[128,512]{1,0:T(8,128)}, f32[1,128]{1,0:T(1,128)}) custom-call(bf16[2,128,512]{2,1,0:T(8,128)(2,1)S(1)} %copy-done.1, bf16[2,128,1536]{2,1,0:T(8,128)(2,1)S(1)} %copy-done, f32[8,128]{1,0:T(8,128)S(1)} %copy-done.2), custom_call_target="tpu_custom_call" | custom-call | tf_op jit(solution)/shard_map/widen/pallas_call | solution.py:709
Async XLA Ops:
  90.6 0.7 copy-start.2
  91.3 1.1 %copy-start = (bf16[2,128,1536]{2,1,0:T(8,128)(2,1)S(1)}, bf16[2,128,1536]{2,1,0:T(8,128)(2,1)}, u32[]{:S(2)}) copy-start(bf16[2,128,1536]{2,1,0:T(8,128)(2,1)} %get-tuple-element.14.total) | copy-start | bytes 2359300
  92.4 0.9 %copy-start.1 = (bf16[2,128,512]{2,1,0:T(8,128)(2,1)S(1)}, bf16[2,128,512]{2,1,0:T(8,128)(2,1)}, u32[]{:S(2)}) copy-start(bf16[2,128,512]{2,1,0:T(8,128)(2,1)} %get-tuple-element.13.home_in) | copy-start | bytes 786436

commit v4 on v3

--- a/solution.py
+++ b/solution.py
@@ -83,16 +83,23 @@
         hop.landed()
 
 
-def add_into(count, dst, terms):
+def add_into(count, step, dst, terms):
     def one(i, carry):
-        at = i * 16
-        value = terms[0](at).astype(F32)
-        for term in terms[1:]:
-            value = value + term(at).astype(F32)
-        dst(at, value.astype(BF))
+        at = i * step
+        if len(terms) == 2:
+            dst(at, terms[0](at) + terms[1](at))
+        else:
+            value = terms[0](at).astype(F32)
+            for term in terms[1:]:
+                value = value + term(at).astype(F32)
+            dst(at, value.astype(BF))
         return carry
 
-    lax.fori_loop(0, count // 16, one, 0)
+    lax.fori_loop(0, count // step, one, 0)
+
+
+def block_rows(count, wide):
+    return min(count, 49152 // wide // 16 * 16)
 
 
 class Ring:
@@ -100,63 +107,64 @@
         self.buf, self.one_in, self.two_in = buf, one_in, two_in
         step = [lax.rem(me + k, 4) for k in range(4)]
         self.rects = [rect(j) for j in step]
-        self.nr = self.rects[0][1]
+        self.nr, self.nc = self.rects[0][1], self.rects[0][3]
         far, after, before = self.rects[2], self.rects[1], self.rects[3]
         half = self.nr // 2
+        top, bottom = pl.ds(0, half), pl.ds(half, half)
         self.one = [
             net.hop(self.view(far, 0, half), one_in.at[0], right),
             net.hop(self.view(far, half, half), one_in.at[1], left),
         ]
+        self.plain = [
+            net.hop(self.view(after, half, half), two_in.at[0, bottom], right),
+            net.hop(self.view(before, 0, half), two_in.at[1, top], left),
+        ]
         self.two = [
-            net.hop(self.view(after, 0, self.nr), two_in.at[0], right),
-            net.hop(self.view(before, 0, self.nr), two_in.at[1], left),
+            net.hop(self.view(after, 0, half), two_in.at[0, top], right),
+            net.hop(self.view(before, half, half), two_in.at[1, bottom], left),
         ]
 
-    def index(self, rect, offset, count):
+    def at(self, rect, offset, count):
         r0, nr, c0, nc = rect
-        first = pl.ds(offset, count) if isinstance(r0, int) else span(r0 + offset, count, 16)
+        first = pl.ds(offset, count) if isinstance(r0, int) and isinstance(offset, int) else span(r0 + offset, count, 16)
         second = pl.ds(0, nc) if isinstance(c0, int) else span(c0, nc, 128)
         return (first, second)
 
     def view(self, rect, offset, count):
-        return self.buf.at[self.index(rect, offset, count)]
-
-    def rows_of(self, rect, base):
-        r0, nr, c0, nc = rect
-
-        def at(i):
-            second = pl.ds(0, nc) if isinstance(c0, int) else span(c0, nc, 128)
-            return (span(r0 + base + i, 16), second)
-
-        return at
+        return self.buf.at[self.at(rect, offset, count)]
 
     def fold(self, which):
         self.one[which].landed()
         half = self.nr // 2
         rect, base = (self.rects[1], 0) if which == 0 else (self.rects[3], half)
-        at = self.rows_of(rect, base)
-        source = self.one_in.at[which]
+        step = block_rows(half, self.nc)
 
         def store(i, value):
-            self.buf[at(i)] = value
-
-        add_into(half, store, [lambda i: self.buf[at(i)], lambda i: source[span(i, 16)]])
+            self.buf[self.at(rect, base + i, step)] = value
+
+        add_into(
+            half,
+            step,
+            store,
+            [lambda i: self.buf[self.at(rect, base + i, step)], lambda i: self.one_in[which, span(i, step, 16)]],
+        )
         self.two[which].start()
 
     def finish(self, dst):
-        landed(self.two)
-        at = self.rows_of(self.rects[0], 0)
+        landed(self.plain + self.two)
+        step = block_rows(self.nr, self.nc)
 
         def store(i, value):
-            dst[span(i, 16)] = value
+            dst[span(i, step, 16)] = value
 
         add_into(
             self.nr,
+            step,
             store,
             [
-                lambda i: self.buf[at(i)],
-                lambda i: self.two_in[0, span(i, 16)],
-                lambda i: self.two_in[1, span(i, 16)],
+                lambda i: self.buf[self.at(self.rects[0], i, step)],
+                lambda i: self.two_in[0, span(i, step, 16)],
+                lambda i: self.two_in[1, span(i, step, 16)],
             ],
         )
 
@@ -183,17 +191,19 @@
 
     def finish(self, dst):
         landed(self.hops)
+        step = block_rows(self.mine[1], self.mine[3])
 
         def store(i, value):
-            dst[span(i, 16)] = value
+            dst[span(i, step, 16)] = value
 
         def term(k):
-            return lambda i: self.came_in[k, span(i, 16)]
+            return lambda i: self.came_in[k, span(i, step, 16)]
 
         add_into(
             self.mine[1],
+            step,
             store,
-            [lambda i: self.buf[self.index(self.mine, i, 16)]] + [term(k) for k in range(3)],
+            [lambda i: self.buf[self.index(self.mine, i, step)]] + [term(k) for k in range(3)],
         )
 
 
@@ -209,6 +219,11 @@
 def z_dev(b, step):
     z, y = b // NY, lax.rem(b, NY)
     return {"band": lax.rem(z + step, NZ) * NY + y}
+
+
+def z_near(b, step):
+    z, y = b // NY, lax.rem(b, NY)
+    return {"band": (z // 4 * 4 + lax.rem(lax.rem(z, 4) + step, 4)) * NY + y}
 
 
 def barrier(devices):
@@ -268,41 +283,55 @@
 
     class Gather:
         def __init__(self, src, dst, size):
-            wide = dst.shape[-1]
-            cols = span(y * (wide // NY), wide // NY)
-            half, quarter = size // 2, size // 4
+            wide = dst.shape[-1] // 4
+            half, quarter, eighth = size // 2, size // 4, size // 8
 
             def block(owner, offset, count):
                 return dst.at[s, span(owner * size + offset, count, count)]
 
-            def strip(owner):
-                return dst.at[s, span(owner * size + half, half), cols]
-
-            top, bottom = pl.ds(0, half), pl.ds(half, half)
-            self.strips = [net.hop(src.at[0, bottom, cols], strip(d), x_dev(d, k)) for k in range(1, NX)]
-            self.right = net.hop(src.at[0, top], block(d, 0, half), x_right)
-            self.left = net.hop(src.at[0, top], block(d, 0, half), x_left)
+            def y_strip(owner):
+                return dst.at[s, span(owner * size + quarter, half, quarter), span(y * wide, wide)]
+
+            def z_strip(owner):
+                return dst.at[
+                    s, span(owner * size + 3 * quarter, quarter), span(lax.rem(z, 4) * wide, wide)
+                ]
+
+            top = pl.ds(0, quarter)
+            y_src = src.at[0, pl.ds(quarter, half), span(y * wide, wide)]
+            z_src = src.at[0, pl.ds(3 * quarter, quarter), span(lax.rem(z, 4) * wide, wide)]
+            self.y_strips = [net.hop(y_src, y_strip(d), x_dev(d, k)) for k in range(1, NX)]
+            self.z_strips = [net.hop(z_src, z_strip(d), x_dev(d, k)) for k in range(1, NX)]
+            self.right = net.hop(src.at[0, top], block(d, 0, quarter), x_right)
+            self.left = net.hop(src.at[0, top], block(d, 0, quarter), x_left)
             self.mine = net.hop(src.at[0], block(d, 0, size), core)
             self.local = net.keep(src.at[0], block(d, 0, size))
-            self.spread = [
-                [net.hop(strip(xd[NX - k]), strip(xd[NX - k]), y_dev(b, m)) for m in range(1, NY)]
-                for k in range(1, NX)
+            owners = [xd[NX - k] for k in range(1, NX)]
+            self.y_spread = [
+                [net.hop(y_strip(o), y_strip(o), y_dev(b, m)) for m in range(1, NY)] for o in owners
             ]
-            self.far_right = net.hop(block(xd[3], 0, quarter), block(xd[3], 0, quarter), x_right)
-            self.far_left = net.hop(block(xd[1], quarter, quarter), block(xd[1], quarter, quarter), x_left)
-            self.across = [
-                net.hop(block(xd[NX - k], 0, size), block(xd[NX - k], 0, size), core)
-                for k in range(1, NX)
+            self.z_spread = [
+                [net.hop(z_strip(o), z_strip(o), z_near(b, m)) for m in range(1, 4)] for o in owners
             ]
-
-        def begin(self):
+            self.far_right = net.hop(block(xd[3], 0, eighth), block(xd[3], 0, eighth), x_right)
+            self.far_left = net.hop(block(xd[1], eighth, eighth), block(xd[1], eighth, eighth), x_left)
+            self.across = [net.hop(block(o, 0, size), block(o, 0, size), core) for o in owners]
+
+        def begin_strips(self):
+            for k in (2, 1, 3):
+                self.y_strips[k - 1].start()
+                self.z_strips[k - 1].start()
+
+        def begin_blocks(self):
             start([self.right, self.left, self.mine])
             self.local.start()
 
         def relay_strips(self):
             for k in (1, 3, 2):
-                self.strips[k - 1].landed()
-                start(self.spread[k - 1])
+                self.y_strips[k - 1].landed()
+                start(self.y_spread[k - 1])
+                self.z_strips[k - 1].landed()
+                start(self.z_spread[k - 1])
 
         def relay(self):
             self.right.landed()
@@ -311,12 +340,12 @@
             self.far_left.start()
 
         def pass_on(self):
-            for k in (1, 3):
-                landed(self.spread[k - 1])
+            for k in (1, 3, 2):
+                landed(self.y_spread[k - 1])
+                landed(self.z_spread[k - 1])
+                if k == 2:
+                    landed([self.far_right, self.far_left])
                 self.across[k - 1].start()
-            landed(self.spread[1])
-            landed([self.far_right, self.far_left])
-            self.across[1].start()
 
         def ready(self):
             landed([self.mine] + self.across)
@@ -368,29 +397,23 @@
     ]
     stays = net.keep(y_ref.at[s, lo], y_home.at[s, hi])
 
+    def core_sum(where, count, wide):
+        step = block_rows(count, wide)
+
+        def store(r, value):
+            mine[where(r, step)] = value
+
+        add_into(
+            count, step, store, [lambda r: mine[where(r, step)], lambda r: core_in[where(r, step)]]
+        )
+
     def a_core(i):
         swap_a[i].landed()
-        base = a_order[i] * TOK
-
-        def at(r):
-            return (0, span(base + r, 16))
-
-        def store(r, value):
-            mine[at(r)] = value
-
-        add_into(TOK, store, [lambda r: mine[at(r)], lambda r: core_in[at(r)]])
+        core_sum(lambda r, step: (0, span(a_order[i] * TOK + r, step, 16)), TOK, WIDE)
 
     def q_core(i):
         swap_q[i].landed()
-        cols = span(q_order[i] * PART, PART, 128)
-
-        def at(r):
-            return (1, span(r, 16), cols)
-
-        def store(r, value):
-            mine[at(r)] = value
-
-        add_into(D, store, [lambda r: mine[at(r)], lambda r: core_in[at(r)]])
+        core_sum(lambda r, step: (1, span(r, step, 16), span(q_order[i] * PART, PART, 128)), D, PART)
 
     def swap():
         for hop_a, hop_q in zip(swap_a, swap_q):
@@ -405,7 +428,9 @@
         start(ring_qy.one)
         for i in (1, 2):
             a_core(i)
+            ring_ax.plain[i - 1].start()
             q_core(i)
+            ring_qy.plain[i - 1].start()
         gain_swap.landed()
         gain_sum[...] = gain_grads[s] + gain_core[...]
         gain_x[0] = gain_sum[d]
@@ -538,14 +563,12 @@
         return gu
 
     for part in (merge, qkv, outw):
-        start(part.strips)
-    start(shift[:2])
-    merge.begin()
-    start(gain_hops + gain_core_hops[:1])
+        part.begin_strips()
+    start(shift[:2] + gain_hops + gain_core_hops[:1])
+    for part in (merge, qkv, outw):
+        part.begin_blocks()
     for copy in own:
         copy.start()
-    qkv.begin()
-    outw.begin()
     shift[2].start()
     for part in (merge, qkv, outw):
         part.relay_strips()
@@ -634,13 +657,20 @@
         hop.sent()
 
 
-def widen(home_in, total, gain_in, home, merge, qkv, out, gain):
-    home[...] = home_in[...]
+def widen(home_in, total_in, gain_in, home, merge, qkv, out, gain, total, sems):
+    copies = [
+        pltpu.make_async_copy(total_in, total, sems.at[0]),
+        pltpu.make_async_copy(home_in, home, sems.at[1]),
+    ]
+    for copy in copies:
+        copy.start()
+    gain[...] = gain_in[0:1]
+    copies[0].wait()
     merge[0:TOK] = total[0, :, 0:D].astype(F32)
     merge[TOK : 2 * TOK] = total[0, :, D : 2 * D].astype(F32)
     out[...] = total[0, :, 2 * D : 3 * D].astype(F32)
     qkv[...] = total[1].astype(F32)
-    gain[...] = gain_in[0:1]
+    copies[1].wait()
 
 
 def vmem(count):
@@ -697,8 +727,8 @@
             pltpu.VMEM((4, 8, TOK), F32),
             pltpu.VMEM((NY, 8, TOK), F32),
             pltpu.VMEM((NZ, 8, TOK), F32),
-            pltpu.SemaphoreType.DMA((176,)),
-            pltpu.SemaphoreType.DMA((176,)),
+            pltpu.SemaphoreType.DMA((224,)),
+            pltpu.SemaphoreType.DMA((224,)),
             pltpu.SemaphoreType.DMA((8,)),
         ],
         compiler_params=pltpu.CompilerParams(
@@ -712,9 +742,10 @@
             shape((2, TOK, D)), shape((2 * TOK, D), F32), shape((TOK, 3 * D), F32),
             shape((TOK, D), F32), shape((1, TOK), F32),
         ),
-        in_specs=vmem(3),
+        in_specs=anywhere(2) + vmem(1),
         out_specs=vmem(5),
-        compiler_params=pltpu.CompilerParams(vmem_limit_bytes=16 * 1024 * 1024),
+        scratch_shapes=[pltpu.VMEM((2, TOK, WIDE), BF), pltpu.SemaphoreType.DMA((2,))],
+        compiler_params=pltpu.CompilerParams(vmem_limit_bytes=VMEM_LIMIT),
         name="widen",
     )(home, total, gain_total)
     section_home = home.reshape(1, 1, 2, 8, 16, D)

time: 95.1 us -> 89.9 us (0.945)
  local copies, waits for them, and re-layouts: 2.76 us -> 0 us
  Pallas kernels: 91.3 us -> 89.1 us
    pallas_call x1, Pallas kernels: 89.9 us -> 86 us  [body(): pl.pallas_call(kernel, out_shape=(shape((2, TOK, D)), shape((2, TOK, WIDE...]
    unnamed x6 -> x0, local copies, waits for them, and re-layouts: 2.76 us -> none
    pallas_call x1, Pallas kernels: 1.33 us -> 3.15 us  [body(): pl.pallas_call(widen, out_shape=(shape((2, TOK, D)), shape((2 * TOK, D),...]
where the time goes in v4:
time: 89.9 us; the launch traced here: 89.8 us
  Pallas kernels  89.1 us (99%)
    pallas_call x1, Pallas kernels, body(): pl.pallas_call(kernel, out_shape=(shape((2, TOK, D)), shape((2, TOK, WIDE...  86 us
    pallas_call x1, Pallas kernels, body(): pl.pallas_call(widen, out_shape=(shape((2, TOK, D)), shape((2 * TOK, D),...  3.15 us

profile of v4, /device:TPU:2, one launch (start us, length us, event | category | flops | bytes accessed | tf_op | source)
XLA Modules:
  0.0 89.8 jit_solution(11094195844381838667)
XLA Ops:
  0.6 86.0 %step.1 = (bf16[2,128,512]{2,1,0:T(8,128)(2,1)}, bf16[2,128,1536]{2,1,0:T(8,128)(2,1)}, f32[8,128]{1,0:T(8,128)}) custom-call(bf16[2,128,512]{2,1,0:T(8,128)(2,1)} %bitcast.7, bf16[2,128,512]{2,1,0:T(8,128)(2,1)} %bitcast.8, s32[2,8,16]{2,1,0:T(8,128)} %bitcast.9, bf16[1,256,512]{2,1,0:T(8,128)(2,1)} %wm_in.1, bf16[1,128,1536]{2,1,0:T(8,128)(2,1)} %wq_in.1, ...), custom_call_target="tpu_custom_call" | custom-call | tf_op jit(solution)/shard_map/step/pallas_call | solution.py:692
  86.6 3.2 %widen.1 = (bf16[2,128,512]{2,1,0:T(8,128)(2,1)}, f32[256,512]{1,0:T(8,128)}, f32[128,1536]{1,0:T(8,128)}, f32[128,512]{1,0:T(8,128)}, f32[1,128]{1,0:T(1,128)}) custom-call(bf16[2,128,512]{2,1,0:T(8,128)(2,1)} %get-tuple-element.13.home_in, bf16[2,128,1536]{2,1,0:T(8,128)(2,1)} %get-tuple-element.14.total_in, f32[8,128]{1,0:T(8,128)} %get-tuple-element.15.gain_in), custom_call_target="tpu_custom_call" | custom-call | tf_op jit(solution)/shard_map/widen/pallas_call | solution.py:739

commit v5 on v4

--- a/solution.py
+++ b/solution.py
@@ -17,6 +17,8 @@
 TALL = TOK // NZ
 EPSILON = 1e-05
 MASKED = -1e30
+SENDS = 22
+RECVS = 88
 VMEM_LIMIT = 58 * 1024 * 1024
 MESH = pl.DeviceIdType.MESH
 BF = jnp.bfloat16
@@ -39,16 +41,23 @@
     return pl.ds(pl.multiple_of(index, unit or size), size)
 
 
+class Group:
+    def __init__(self, sem, size_ref):
+        self.sem, self.size_ref = sem, size_ref
+
+    def wait(self):
+        pltpu.make_async_copy(self.size_ref, self.size_ref, self.sem).wait()
+
+
 class Hop:
-    def __init__(self, net, src, dst, device):
-        at = net.used
-        net.used += 1
-        net.hops.append(self)
+    def __init__(self, net, src, dst, device, send, recv):
+        if send is None:
+            net.alone.append(self)
         self.copy = pltpu.make_async_remote_copy(
             src_ref=src,
             dst_ref=dst,
-            send_sem=net.send.at[at],
-            recv_sem=net.recv.at[at],
+            send_sem=send.sem if send else net.send_sem(),
+            recv_sem=recv.sem if recv else net.recv_sem(),
             device_id=device,
             device_id_type=MESH,
         )
@@ -60,17 +69,41 @@
 class Net:
     def __init__(self, send, recv, local):
         self.send, self.recv, self.local = send, recv, local
-        self.used = 0
+        self.sends = 0
+        self.recvs = 0
         self.kept = 0
-        self.hops = []
-
-    def hop(self, src, dst, device):
-        return Hop(self, src, dst, device)
+        self.alone = []
+        self.groups = []
+
+    def send_sem(self):
+        self.sends += 1
+        return self.send.at[self.sends - 1]
+
+    def recv_sem(self):
+        self.recvs += 1
+        return self.recv.at[self.recvs - 1]
+
+    def sending(self, size_ref):
+        group = Group(self.send_sem(), size_ref)
+        self.groups.append(group)
+        return group
+
+    def landing(self, size_ref):
+        return Group(self.recv_sem(), size_ref)
+
+    def hop(self, src, dst, device, send=None, recv=None):
+        return Hop(self, src, dst, device, send, recv)
 
     def keep(self, src, dst):
         copy = pltpu.make_async_copy(src, dst, self.local.at[self.kept])
         self.kept += 1
         return copy
+
+    def drain(self):
+        for hop in self.alone:
+            hop.sent()
+        for group in self.groups:
+            group.wait()
 
 
 def start(hops):
@@ -103,7 +136,7 @@
 
 
 class Ring:
-    def __init__(self, net, buf, rect, me, right, left, one_in, two_in):
+    def __init__(self, net, buf, rect, me, right, left, one_in, two_in, sent_ref):
         self.buf, self.one_in, self.two_in = buf, one_in, two_in
         step = [lax.rem(me + k, 4) for k in range(4)]
         self.rects = [rect(j) for j in step]
@@ -111,17 +144,19 @@
         far, after, before = self.rects[2], self.rects[1], self.rects[3]
         half = self.nr // 2
         top, bottom = pl.ds(0, half), pl.ds(half, half)
+        out = net.sending(sent_ref)
+        self.came = net.landing(two_in)
         self.one = [
-            net.hop(self.view(far, 0, half), one_in.at[0], right),
-            net.hop(self.view(far, half, half), one_in.at[1], left),
+            net.hop(self.view(far, 0, half), one_in.at[0], right, out),
+            net.hop(self.view(far, half, half), one_in.at[1], left, out),
         ]
         self.plain = [
-            net.hop(self.view(after, half, half), two_in.at[0, bottom], right),
-            net.hop(self.view(before, 0, half), two_in.at[1, top], left),
+            net.hop(self.view(after, half, half), two_in.at[0, bottom], right, out, self.came),
+            net.hop(self.view(before, 0, half), two_in.at[1, top], left, out, self.came),
         ]
         self.two = [
-            net.hop(self.view(after, 0, half), two_in.at[0, top], right),
-            net.hop(self.view(before, half, half), two_in.at[1, bottom], left),
+            net.hop(self.view(after, 0, half), two_in.at[0, top], right, out, self.came),
+            net.hop(self.view(before, half, half), two_in.at[1, bottom], left, out, self.came),
         ]
 
     def at(self, rect, offset, count):
@@ -151,7 +186,7 @@
         self.two[which].start()
 
     def finish(self, dst):
-        landed(self.plain + self.two)
+        self.came.wait()
         step = block_rows(self.nr, self.nc)
 
         def store(i, value):
@@ -173,8 +208,9 @@
     def __init__(self, net, buf, rect, me, peer, came_in):
         self.buf, self.came_in = buf, came_in
         self.mine = rect(me)
+        out, self.came = net.sending(came_in), net.landing(came_in)
         self.hops = [
-            net.hop(buf.at[self.index(rect(lax.rem(me + k, 4)), 0, None)], came_in.at[k - 1], peer(k))
+            net.hop(buf.at[self.index(rect(lax.rem(me + k, 4)), 0, None)], came_in.at[k - 1], peer(k), out, self.came)
             for k in range(1, 4)
         ]
 
@@ -190,7 +226,7 @@
             self.hops[k - 1].start()
 
     def finish(self, dst):
-        landed(self.hops)
+        self.came.wait()
         step = block_rows(self.mine[1], self.mine[3])
 
         def store(i, value):
@@ -276,13 +312,19 @@
         net.keep(g_in.at[s, hi], cot_ref.at[lo]),
     ]
     gain[s, d] = jnp.broadcast_to(gain_in[...].astype(F32), (8, TOK))
-    gain_hops = [net.hop(gain.at[s, d], gain.at[s, d], x_dev(d, k)) for k in range(1, NX)]
-    gain_core_hops = [net.hop(gain.at[s, xd[0]], gain.at[s, xd[0]], core)] + [
-        net.hop(gain.at[s, xd[NX - k]], gain.at[s, xd[NX - k]], core) for k in range(1, NX)
+    seven = gain_z.at[pl.ds(0, 7)]
+    gain_out, gain_in_all = net.sending(seven), net.landing(gain.at[0, pl.ds(0, 3)])
+    gain_in_core = net.landing(gain.at[0])
+    gain_hops = [
+        net.hop(gain.at[s, d], gain.at[s, d], x_dev(d, k), gain_out, gain_in_all) for k in range(1, NX)
+    ]
+    gain_core_hops = [net.hop(gain.at[s, xd[0]], gain.at[s, xd[0]], core, gain_out, gain_in_core)] + [
+        net.hop(gain.at[s, xd[NX - k]], gain.at[s, xd[NX - k]], core, gain_out, gain_in_core)
+        for k in range(1, NX)
     ]
 
     class Gather:
-        def __init__(self, src, dst, size):
+        def __init__(self, src, dst, size, sent_ref):
             wide = dst.shape[-1] // 4
             half, quarter, eighth = size // 2, size // 4, size // 8
 
@@ -300,22 +342,32 @@
             top = pl.ds(0, quarter)
             y_src = src.at[0, pl.ds(quarter, half), span(y * wide, wide)]
             z_src = src.at[0, pl.ds(3 * quarter, quarter), span(lax.rem(z, 4) * wide, wide)]
-            self.y_strips = [net.hop(y_src, y_strip(d), x_dev(d, k)) for k in range(1, NX)]
-            self.z_strips = [net.hop(z_src, z_strip(d), x_dev(d, k)) for k in range(1, NX)]
-            self.right = net.hop(src.at[0, top], block(d, 0, quarter), x_right)
-            self.left = net.hop(src.at[0, top], block(d, 0, quarter), x_left)
-            self.mine = net.hop(src.at[0], block(d, 0, size), core)
+            out = net.sending(sent_ref)
+            self.y_strips = [net.hop(y_src, y_strip(d), x_dev(d, k), out) for k in range(1, NX)]
+            self.z_strips = [net.hop(z_src, z_strip(d), x_dev(d, k), out) for k in range(1, NX)]
+            self.right = net.hop(src.at[0, top], block(d, 0, quarter), x_right, out)
+            self.left = net.hop(src.at[0, top], block(d, 0, quarter), x_left, out)
+            self.from_core = net.landing(dst.at[0])
+            self.mine = net.hop(src.at[0], block(d, 0, size), core, out, self.from_core)
             self.local = net.keep(src.at[0], block(d, 0, size))
             owners = [xd[NX - k] for k in range(1, NX)]
+            others = pl.ds(0, 3 * wide)
+            self.y_came = [net.landing(dst.at[0, pl.ds(0, half), others]) for o in owners]
+            self.z_came = [net.landing(dst.at[0, pl.ds(0, quarter), others]) for o in owners]
             self.y_spread = [
-                [net.hop(y_strip(o), y_strip(o), y_dev(b, m)) for m in range(1, NY)] for o in owners
+                [net.hop(y_strip(o), y_strip(o), y_dev(b, m), out, came) for m in range(1, NY)]
+                for o, came in zip(owners, self.y_came)
             ]
             self.z_spread = [
-                [net.hop(z_strip(o), z_strip(o), z_near(b, m)) for m in range(1, 4)] for o in owners
+                [net.hop(z_strip(o), z_strip(o), z_near(b, m), out, came) for m in range(1, 4)]
+                for o, came in zip(owners, self.z_came)
             ]
-            self.far_right = net.hop(block(xd[3], 0, eighth), block(xd[3], 0, eighth), x_right)
-            self.far_left = net.hop(block(xd[1], eighth, eighth), block(xd[1], eighth, eighth), x_left)
-            self.across = [net.hop(block(o, 0, size), block(o, 0, size), core) for o in owners]
+            self.far_right = net.hop(block(xd[3], 0, eighth), block(xd[3], 0, eighth), x_right, out)
+            self.far_left = net.hop(block(xd[1], eighth, eighth), block(xd[1], eighth, eighth), x_left, out)
+            self.across = [
+                net.hop(block(o, 0, size), block(o, 0, size), core, out, self.from_core)
+                for o in owners
+            ]
 
         def begin_strips(self):
             for k in (2, 1, 3):
@@ -341,19 +393,19 @@
 
         def pass_on(self):
             for k in (1, 3, 2):
-                landed(self.y_spread[k - 1])
-                landed(self.z_spread[k - 1])
+                self.y_came[k - 1].wait()
+                self.z_came[k - 1].wait()
                 if k == 2:
                     landed([self.far_right, self.far_left])
                 self.across[k - 1].start()
 
         def ready(self):
-            landed([self.mine] + self.across)
+            self.from_core.wait()
             self.local.wait()
 
-    merge = Gather(wm_in, wm, 2 * TOK)
-    qkv = Gather(wq_in, wq, TOK)
-    outw = Gather(wo_in, wo, TOK)
+    merge = Gather(wm_in, wm, 2 * TOK, grads.at[:, :, pl.ds(0, 448), pl.ds(0, D)])
+    qkv = Gather(wq_in, wq, TOK, grads.at[0, :, pl.ds(0, 448)])
+    outw = Gather(wo_in, wo, TOK, grads.at[0, :, pl.ds(0, 448), pl.ds(0, D)])
 
     mine = grads.at[s]
     theirs = grads.at[other]
@@ -366,21 +418,36 @@
     def q_cols(j):
         return (1, pl.ds(0, D), span(j * PART, PART, 128))
 
-    swap_a = [net.hop(theirs.at[a_rows(j)], core_in.at[a_rows(j)], core) for j in a_order]
-    swap_q = [net.hop(theirs.at[q_cols(j)], core_in.at[q_cols(j)], core) for j in q_order]
+    out = net.sending(core_in)
+    swap_a = [net.hop(theirs.at[a_rows(j)], core_in.at[a_rows(j)], core, out) for j in a_order]
+    swap_q = [net.hop(theirs.at[q_cols(j)], core_in.at[q_cols(j)], core, out) for j in q_order]
     gain_swap = net.hop(gain_grads.at[other], gain_core, core)
-    ring_ax = Ring(net, mine.at[0], lambda j: (j * TOK, TOK, 0, WIDE), d, x_right, x_left, ax_one, ax_two)
-    ring_qy = Ring(net, mine.at[1], lambda j: (0, D, j * PART, PART), y, y_right, y_left, qy_one, qy_two)
+    ring_ax = Ring(net, mine.at[0], lambda j: (j * TOK, TOK, 0, WIDE), d, x_right, x_left, ax_one, ax_two,
+                   core_in.at[0, pl.ds(0, 3 * TOK)])
+    ring_qy = Ring(net, mine.at[1], lambda j: (0, D, j * PART, PART), y, y_right, y_left, qy_one, qy_two,
+                   core_in.at[0, :, pl.ds(0, 3 * PART)])
     to_ay = Direct(net, a_sum, lambda j: (0, TOK, j * PART, PART), y, lambda k: y_dev(b, k), ay_in)
     to_qx = Direct(net, q_sum, lambda j: (j * TOK, TOK, 0, PART), d, lambda k: x_dev(d, k), qx_in)
-    gain_x_hops = [net.hop(gain_sum.at[xd[k]], gain_x.at[k], x_dev(d, k)) for k in range(1, NX)]
-    gain_y_hops = [net.hop(gain_y.at[0], gain_y.at[k], y_dev(b, k)) for k in range(1, NY)]
-    gain_z_hops = [net.hop(gain_z.at[0], gain_z.at[k], z_dev(b, k)) for k in range(1, NZ)]
+    three = gain_x.at[pl.ds(0, 3)]
+    out, gain_x_in = net.sending(three), net.landing(three)
+    gain_x_hops = [
+        net.hop(gain_sum.at[xd[k]], gain_x.at[k], x_dev(d, k), out, gain_x_in) for k in range(1, NX)
+    ]
+    out, gain_y_in = net.sending(three), net.landing(three)
+    gain_y_hops = [
+        net.hop(gain_y.at[0], gain_y.at[k], y_dev(b, k), out, gain_y_in) for k in range(1, NY)
+    ]
+    out, gain_z_in = net.sending(seven), net.landing(seven)
+    gain_z_hops = [
+        net.hop(gain_z.at[0], gain_z.at[k], z_dev(b, k), out, gain_z_in) for k in range(1, NZ)
+    ]
     z_rows = span(z * TALL, TALL)
     both = pl.ds(0, 2)
+    seven_pieces = z_in.at[pl.ds(0, 7)]
+    out, z_came = net.sending(seven_pieces), net.landing(seven_pieces)
     z_hops = [
         net.hop(
-            y_sum.at[both, span(lax.rem(z + k, NZ) * TALL, TALL)], z_in.at[k], z_dev(b, k)
+            y_sum.at[both, span(lax.rem(z + k, NZ) * TALL, TALL)], z_in.at[k], z_dev(b, k), out, z_came
         )
         for k in range(1, NZ)
     ]
@@ -388,8 +455,14 @@
         at = (both, span(lax.rem(z + NZ - k, NZ) * TALL, TALL), span(y * PART, PART, 128))
         return total.at[at]
 
-    z_back = [net.hop(piece(0), piece(0), z_dev(b, k)) for k in range(1, NZ)]
-    y_back = [[net.hop(piece(k), piece(k), y_dev(b, m)) for m in range(1, NY)] for k in range(NZ)]
+    out = net.sending(seven_pieces)
+    z_back = [net.hop(piece(0), piece(0), z_dev(b, k), out) for k in range(1, NZ)]
+    three_parts = total.at[both, pl.ds(0, TOK), pl.ds(0, 3 * PART)]
+    out, y_came = net.sending(three_parts), net.landing(three_parts)
+    y_back = [
+        [net.hop(piece(k), piece(k), y_dev(b, m), out, y_came) for m in range(1, NY)]
+        for k in range(NZ)
+    ]
     home = [
         net.hop(y_ref.at[other, lo], y_home.at[s, hi], core),
         net.hop(y_ref.at[s, hi], y_home.at[s, lo], {"band": nxt}),
@@ -442,7 +515,7 @@
             ring_qy.fold(which)
         a_core(3)
         q_core(3)
-        landed(gain_x_hops)
+        gain_x_in.wait()
         gain_y[0] = (gain_x[0] + gain_x[1]) + (gain_x[2] + gain_x[3])
         start(gain_y_hops)
 
@@ -451,7 +524,7 @@
         to_ay.begin()
         ring_qy.finish(q_sum)
         to_qx.begin()
-        landed(gain_y_hops)
+        gain_y_in.wait()
         gain_z[0] = (gain_y[0] + gain_y[1]) + (gain_y[2] + gain_y[3])
         start(gain_z_hops)
 
@@ -574,11 +647,10 @@
         part.relay_strips()
     merge.relay()
     qkv.relay()
-    for k in range(1, NX):
-        gain_hops[k - 1].landed()
-        gain_core_hops[k].start()
+    gain_in_all.wait()
+    start(gain_core_hops[1:])
     merge.pass_on()
-    landed(gain_core_hops)
+    gain_in_core.wait()
     landed(shift)
     for copy in own:
         copy.wait()
@@ -634,13 +706,13 @@
     to_qx.finish(y_sum.at[1])
     start(z_hops)
     value = y_sum[both, z_rows].astype(F32)
+    z_came.wait()
     for k in range(1, NZ):
-        z_hops[k - 1].landed()
         value = value + z_in[k].astype(F32)
     total[both, z_rows, span(y * PART, PART, 128)] = value.astype(BF)
     start(z_back)
     start(y_back[0])
-    landed(gain_z_hops)
+    gain_z_in.wait()
     gain_value = gain_z[0]
     for k in range(1, NZ):
         gain_value = gain_value + gain_z[k]
@@ -651,26 +723,17 @@
             start(y_back[k])
     landed(home)
     stays.wait()
-    for hops in y_back:
-        landed(hops)
-    for hop in net.hops:
-        hop.sent()
-
-
-def widen(home_in, total_in, gain_in, home, merge, qkv, out, gain, total, sems):
-    copies = [
-        pltpu.make_async_copy(total_in, total, sems.at[0]),
-        pltpu.make_async_copy(home_in, home, sems.at[1]),
-    ]
-    for copy in copies:
-        copy.start()
-    gain[...] = gain_in[0:1]
-    copies[0].wait()
-    merge[0:TOK] = total[0, :, 0:D].astype(F32)
-    merge[TOK : 2 * TOK] = total[0, :, D : 2 * D].astype(F32)
+    y_came.wait()
+    net.drain()
+
+
+def widen(home_in, total, gain_in, home, merge, qkv, out, gain):
+    home[...] = home_in[...]
+    merge[0] = total[0, :, 0:D].astype(F32)
+    merge[1] = total[0, :, D : 2 * D].astype(F32)
     out[...] = total[0, :, 2 * D : 3 * D].astype(F32)
     qkv[...] = total[1].astype(F32)
-    copies[1].wait()
+    gain[...] = gain_in[0:1]
 
 
 def vmem(count):
@@ -727,9 +790,9 @@
             pltpu.VMEM((4, 8, TOK), F32),
             pltpu.VMEM((NY, 8, TOK), F32),
             pltpu.VMEM((NZ, 8, TOK), F32),
-            pltpu.SemaphoreType.DMA((224,)),
-            pltpu.SemaphoreType.DMA((224,)),
-            pltpu.SemaphoreType.DMA((8,)),
+            pltpu.SemaphoreType.DMA((SENDS,)),
+            pltpu.SemaphoreType.DMA((RECVS,)),
+            pltpu.SemaphoreType.DMA((7,)),
         ],
         compiler_params=pltpu.CompilerParams(
             collective_id=0, has_side_effects=True, vmem_limit_bytes=VMEM_LIMIT
@@ -738,16 +801,27 @@
     )(x_in, g_in, use, merge_weight, qkv_weight, out_weight, norm_gain)
     home, merge_grad, qkv_grad, out_grad, gain_grad = pl.pallas_call(
         widen,
+        grid=(2,),
         out_shape=(
-            shape((2, TOK, D)), shape((2 * TOK, D), F32), shape((TOK, 3 * D), F32),
+            shape((2, TOK, D)), shape((2, TOK, D), F32), shape((TOK, 3 * D), F32),
             shape((TOK, D), F32), shape((1, TOK), F32),
         ),
-        in_specs=anywhere(2) + vmem(1),
-        out_specs=vmem(5),
-        scratch_shapes=[pltpu.VMEM((2, TOK, WIDE), BF), pltpu.SemaphoreType.DMA((2,))],
+        in_specs=[
+            pl.BlockSpec((2, 64, D), lambda i: (0, i, 0)),
+            pl.BlockSpec((2, 64, WIDE), lambda i: (0, i, 0)),
+            pl.BlockSpec((8, TOK), lambda i: (0, 0)),
+        ],
+        out_specs=[
+            pl.BlockSpec((2, 64, D), lambda i: (0, i, 0)),
+            pl.BlockSpec((2, 64, D), lambda i: (0, i, 0)),
+            pl.BlockSpec((64, 3 * D), lambda i: (i, 0)),
+            pl.BlockSpec((64, D), lambda i: (i, 0)),
+            pl.BlockSpec((1, TOK), lambda i: (0, 0)),
+        ],
         compiler_params=pltpu.CompilerParams(vmem_limit_bytes=VMEM_LIMIT),
         name="widen",
     )(home, total, gain_total)
+    merge_grad = merge_grad.reshape(2 * TOK, D)
     section_home = home.reshape(1, 1, 2, 8, 16, D)
     return (section_home, merge_grad[None], qkv_grad[None], out_grad[None], gain_grad)
 

time: 89.9 us -> 85.8 us (0.954)
  Pallas kernels: 89.1 us -> 85 us
    pallas_call x1, Pallas kernels: 86 us -> 82.7 us  [body(): pl.pallas_call(kernel, out_shape=(shape((2, TOK, D)), shape((2, TOK, WIDE...]
where the time goes in v5:
time: 85.8 us; the launch traced here: 85.7 us
  Pallas kernels  85 us (99%)
    pallas_call x1, Pallas kernels, body(): pl.pallas_call(kernel, out_shape=(shape((2, TOK, D)), shape((2, TOK, WIDE...  82.7 us
    pallas_call x1, Pallas kernels, body(): pl.pallas_call(widen, grid=(2,), out_shape=(shape((2, TOK, D)), shape((2,...  2.38 us

profile of v5, /device:TPU:2, one launch (start us, length us, event | category | flops | bytes accessed | tf_op | source)
XLA Modules:
  0.0 85.7 jit_solution(1505750801175906858)
XLA Ops:
  0.6 82.7 %step.1 = (bf16[2,128,512]{2,1,0:T(8,128)(2,1)}, bf16[2,128,1536]{2,1,0:T(8,128)(2,1)}, f32[8,128]{1,0:T(8,128)}) custom-call(bf16[2,128,512]{2,1,0:T(8,128)(2,1)} %bitcast.7, bf16[2,128,512]{2,1,0:T(8,128)(2,1)} %bitcast.8, s32[2,8,16]{2,1,0:T(8,128)} %bitcast.9, bf16[1,256,512]{2,1,0:T(8,128)(2,1)} %wm_in.1, bf16[1,128,1536]{2,1,0:T(8,128)(2,1)} %wq_in.1, ...), custom_call_target="tpu_custom_call" | custom-call | tf_op jit(solution)/shard_map/step/pallas_call | solution.py:755
  83.3 2.4 %widen.1 = (bf16[2,128,512]{2,1,0:T(8,128)(2,1)}, f32[2,128,512]{2,1,0:T(8,128)}, f32[128,1536]{1,0:T(8,128)}, f32[128,512]{1,0:T(8,128)}, f32[1,128]{1,0:T(1,128)}) custom-call(bf16[2,128,512]{2,1,0:T(8,128)(2,1)} %get-tuple-element.13.home_in, bf16[2,128,1536]{2,1,0:T(8,128)(2,1)} %get-tuple-element.14.total, f32[8,128]{1,0:T(8,128)} %get-tuple-element.15.gain_in), custom_call_target="tpu_custom_call" | custom-call | tf_op jit(solution)/shard_map/widen/pallas_call | solution.py:802

commit v6 on v5

--- a/solution.py
+++ b/solution.py
@@ -446,10 +446,14 @@
     seven_pieces = z_in.at[pl.ds(0, 7)]
     out, z_came = net.sending(seven_pieces), net.landing(seven_pieces)
     z_hops = [
-        net.hop(
-            y_sum.at[both, span(lax.rem(z + k, NZ) * TALL, TALL)], z_in.at[k], z_dev(b, k), out, z_came
-        )
-        for k in range(1, NZ)
+        [
+            net.hop(
+                y_sum.at[which, span(lax.rem(z + k, NZ) * TALL, TALL)], z_in.at[k, which],
+                z_dev(b, k), out, z_came,
+            )
+            for k in (4, 3, 5, 2, 6, 1, 7)[-(NZ - 1):]
+        ]
+        for which in (0, 1)
     ]
     def piece(k):
         at = (both, span(lax.rem(z + NZ - k, NZ) * TALL, TALL), span(y * PART, PART, 128))
@@ -645,11 +649,12 @@
     shift[2].start()
     for part in (merge, qkv, outw):
         part.relay_strips()
-    merge.relay()
-    qkv.relay()
+    for part in (merge, qkv, outw):
+        part.relay()
     gain_in_all.wait()
     start(gain_core_hops[1:])
     merge.pass_on()
+    qkv.pass_on()
     gain_in_core.wait()
     landed(shift)
     for copy in own:
@@ -658,11 +663,9 @@
     x0 = x_ref[...]
     merge.ready()
     update0, inverse0 = forward_merge(0, x0)
-    outw.relay()
-    qkv.pass_on()
+    outw.pass_on()
     qkv.ready()
     forward_attend(0, allowed)
-    outw.pass_on()
     outw.ready()
     y0 = forward_out(0, update0)
     update1, inverse1 = forward_merge(1, y0)
@@ -682,11 +685,11 @@
     side = dot_nt(gu1, wm[1, D : 2 * D]).astype(BF).astype(F32)
     g0 = (chain + side).astype(BF)
 
+    backward_attend(0, g0)
+
     @pl.when(s == 1)
     def _():
         stage1()
-
-    backward_attend(0, g0)
 
     backward_terms(0, x0, g0, inverse0)
 
@@ -703,8 +706,9 @@
         stage3()
 
     to_ay.finish(y_sum.at[0])
+    start(z_hops[0])
     to_qx.finish(y_sum.at[1])
-    start(z_hops)
+    start(z_hops[1])
     value = y_sum[both, z_rows].astype(F32)
     z_came.wait()
     for k in range(1, NZ):

time: 85.8 us -> 82.1 us (0.957)
  Pallas kernels: 85 us -> 80.5 us
    pallas_call x1, Pallas kernels: 82.7 us -> 78.1 us  [body(): pl.pallas_call(kernel, out_shape=(shape((2, TOK, D)), shape((2, TOK, WIDE...]
where the time goes in v6:
time: 82.1 us; the launch traced here: 81.1 us
  Pallas kernels  80.5 us (98%)
    pallas_call x1, Pallas kernels, body(): pl.pallas_call(kernel, out_shape=(shape((2, TOK, D)), shape((2, TOK, WIDE...  78.1 us
    pallas_call x1, Pallas kernels, body(): pl.pallas_call(widen, grid=(2,), out_shape=(shape((2, TOK, D)), shape((2,...  2.38 us

profile of v6, /device:TPU:2, one launch (start us, length us, event | category | flops | bytes accessed | tf_op | source)
XLA Modules:
  0.0 81.1 jit_solution(13675514338231766453)
XLA Ops:
  0.6 78.1 %step.1 = (bf16[2,128,512]{2,1,0:T(8,128)(2,1)}, bf16[2,128,1536]{2,1,0:T(8,128)(2,1)}, f32[8,128]{1,0:T(8,128)}) custom-call(bf16[2,128,512]{2,1,0:T(8,128)(2,1)} %bitcast.7, bf16[2,128,512]{2,1,0:T(8,128)(2,1)} %bitcast.8, s32[2,8,16]{2,1,0:T(8,128)} %bitcast.9, bf16[1,256,512]{2,1,0:T(8,128)(2,1)} %wm_in.1, bf16[1,128,1536]{2,1,0:T(8,128)(2,1)} %wq_in.1, ...), custom_call_target="tpu_custom_call" | custom-call | tf_op jit(solution)/shard_map/step/pallas_call | solution.py:759
  78.8 2.4 %widen.1 = (bf16[2,128,512]{2,1,0:T(8,128)(2,1)}, f32[2,128,512]{2,1,0:T(8,128)}, f32[128,1536]{1,0:T(8,128)}, f32[128,512]{1,0:T(8,128)}, f32[1,128]{1,0:T(1,128)}) custom-call(bf16[2,128,512]{2,1,0:T(8,128)(2,1)} %get-tuple-element.13.home_in, bf16[2,128,1536]{2,1,0:T(8,128)(2,1)} %get-tuple-element.14.total, f32[8,128]{1,0:T(8,128)} %get-tuple-element.15.gain_in), custom_call_target="tpu_custom_call" | custom-call | tf_op jit(solution)/shard_map/widen/pallas_call | solution.py:806

commit v7 on v6

--- a/solution.py
+++ b/solution.py
@@ -686,16 +686,12 @@
     g0 = (chain + side).astype(BF)
 
     backward_attend(0, g0)
-
-    @pl.when(s == 1)
-    def _():
-        stage1()
-
     backward_terms(0, x0, g0, inverse0)
 
     @pl.when(s == 1)
     def _():
         swap()
+        stage1()
         stage2()
         stage3()
 

time: 82.1 us -> 81.5 us (level); the launches traced: 81.1 us -> 81.4 us
  no operation moved by 1% of the time
where the time goes in v7:
time: 81.5 us; the launch traced here: 81.4 us
  Pallas kernels  80.7 us (99%)
    pallas_call x1, Pallas kernels, body(): pl.pallas_call(kernel, out_shape=(shape((2, TOK, D)), shape((2, TOK, WIDE...  78.4 us
    pallas_call x1, Pallas kernels, body(): pl.pallas_call(widen, grid=(2,), out_shape=(shape((2, TOK, D)), shape((2,...  2.38 us

profile of v7, /device:TPU:2, one launch (start us, length us, event | category | flops | bytes accessed | tf_op | source)
XLA Modules:
  0.0 81.4 jit_solution(4354541115507240960)
XLA Ops:
  0.6 78.4 %step.1 = (bf16[2,128,512]{2,1,0:T(8,128)(2,1)}, bf16[2,128,1536]{2,1,0:T(8,128)(2,1)}, f32[8,128]{1,0:T(8,128)}) custom-call(bf16[2,128,512]{2,1,0:T(8,128)(2,1)} %bitcast.7, bf16[2,128,512]{2,1,0:T(8,128)(2,1)} %bitcast.8, s32[2,8,16]{2,1,0:T(8,128)} %bitcast.9, bf16[1,256,512]{2,1,0:T(8,128)(2,1)} %wm_in.1, bf16[1,128,1536]{2,1,0:T(8,128)(2,1)} %wq_in.1, ...), custom_call_target="tpu_custom_call" | custom-call | tf_op jit(solution)/shard_map/step/pallas_call | solution.py:755
  79.0 2.4 %widen.1 = (bf16[2,128,512]{2,1,0:T(8,128)(2,1)}, f32[2,128,512]{2,1,0:T(8,128)}, f32[128,1536]{1,0:T(8,128)}, f32[128,512]{1,0:T(8,128)}, f32[1,128]{1,0:T(1,128)}) custom-call(bf16[2,128,512]{2,1,0:T(8,128)(2,1)} %get-tuple-element.13.home_in, bf16[2,128,1536]{2,1,0:T(8,128)(2,1)} %get-tuple-element.14.total, f32[8,128]{1,0:T(8,128)} %get-tuple-element.15.gain_in), custom_call_target="tpu_custom_call" | custom-call | tf_op jit(solution)/shard_map/widen/pallas_call | solution.py:802

commit v8 on v7

--- a/solution.py
+++ b/solution.py
@@ -493,16 +493,14 @@
         core_sum(lambda r, step: (1, span(r, step, 16), span(q_order[i] * PART, PART, 128)), D, PART)
 
     def swap():
-        for hop_a, hop_q in zip(swap_a, swap_q):
-            hop_a.start()
-            hop_q.start()
+        start(swap_a)
         gain_swap.start()
 
     def stage1():
+        q_core(0)
+        start(ring_qy.one)
         a_core(0)
         start(ring_ax.one)
-        q_core(0)
-        start(ring_qy.one)
         for i in (1, 2):
             a_core(i)
             ring_ax.plain[i - 1].start()
@@ -632,12 +630,16 @@
         ).astype(BF)
         for c in range(4):
             part = slice(TOK * c, TOK * (c + 1))
-            grads[sec, 1, part] = dot_tn(hidden_ref[sec, :, part], dproj_ref[...]).astype(BF)
             grads[sec, 0, part, 2 * D : 3 * D] = dot_tn(mix_ref[sec, :, part], g).astype(BF)
             term = dot_tn(x[:, part], gu).astype(BF)
             for j in (c // 2, c // 2 + 2):
                 grads[sec, 0, TOK * j : TOK * (j + 1), D * (c % 2) : D * (c % 2 + 1)] = term
         return gu
+
+    def backward_qkv(sec):
+        for c in range(4):
+            part = slice(TOK * c, TOK * (c + 1))
+            grads[sec, 1, part] = dot_tn(hidden_ref[sec, :, part], dproj_ref[...]).astype(BF)
 
     for part in (merge, qkv, outw):
         part.begin_strips()
@@ -675,6 +677,8 @@
     stays.start()
     cot = cot_ref[...]
     backward_attend(1, cot)
+    backward_qkv(1)
+    pl.when(s == 0)(lambda: start(swap_q))
     gu1 = backward_terms(1, y0, cot, inverse1)
 
     @pl.when(s == 0)
@@ -686,6 +690,8 @@
     g0 = (chain + side).astype(BF)
 
     backward_attend(0, g0)
+    backward_qkv(0)
+    pl.when(s == 1)(lambda: start(swap_q))
     backward_terms(0, x0, g0, inverse0)
 
     @pl.when(s == 1)

time: 81.5 us -> 83.1 us (1.020)
  Pallas kernels: 80.7 us -> 81.8 us
    pallas_call x1, Pallas kernels: 78.4 us -> 79.4 us  [body(): pl.pallas_call(kernel, out_shape=(shape((2, TOK, D)), shape((2, TOK, WIDE...]
where the time goes in v8:
time: 83.1 us; the launch traced here: 82.4 us
  Pallas kernels  81.8 us (98%)
    pallas_call x1, Pallas kernels, body(): pl.pallas_call(kernel, out_shape=(shape((2, TOK, D)), shape((2, TOK, WIDE...  79.4 us
    pallas_call x1, Pallas kernels, body(): pl.pallas_call(widen, grid=(2,), out_shape=(shape((2, TOK, D)), shape((2,...  2.38 us

profile of v8, /device:TPU:2, one launch (start us, length us, event | category | flops | bytes accessed | tf_op | source)
XLA Modules:
  0.0 82.4 jit_solution(4055649619081003442)
XLA Ops:
  0.6 79.4 %step.1 = (bf16[2,128,512]{2,1,0:T(8,128)(2,1)}, bf16[2,128,1536]{2,1,0:T(8,128)(2,1)}, f32[8,128]{1,0:T(8,128)}) custom-call(bf16[2,128,512]{2,1,0:T(8,128)(2,1)} %bitcast.7, bf16[2,128,512]{2,1,0:T(8,128)(2,1)} %bitcast.8, s32[2,8,16]{2,1,0:T(8,128)} %bitcast.9, bf16[1,256,512]{2,1,0:T(8,128)(2,1)} %wm_in.1, bf16[1,128,1536]{2,1,0:T(8,128)(2,1)} %wq_in.1, ...), custom_call_target="tpu_custom_call" | custom-call | tf_op jit(solution)/shard_map/step/pallas_call | solution.py:761
  80.0 2.4 %widen.1 = (bf16[2,128,512]{2,1,0:T(8,128)(2,1)}, f32[2,128,512]{2,1,0:T(8,128)}, f32[128,1536]{1,0:T(8,128)}, f32[128,512]{1,0:T(8,128)}, f32[1,128]{1,0:T(1,128)}) custom-call(bf16[2,128,512]{2,1,0:T(8,128)(2,1)} %get-tuple-element.13.home_in, bf16[2,128,1536]{2,1,0:T(8,128)(2,1)} %get-tuple-element.14.total, f32[8,128]{1,0:T(8,128)} %get-tuple-element.15.gain_in), custom_call_target="tpu_custom_call" | custom-call | tf_op jit(solution)/shard_map/widen/pallas_call | solution.py:808
